TPU v7x, 32 devices: a whole 2x2x4 slice. The times are simulated.
32 devices in a mesh: gx: 8 (over z, y), gz: 4 (over x, core).
Axes of the slice: x: 2, y: 2, z: 4, core: 2. Of those that a mesh axis runs over, the one named last changes fastest.
Arguments:
- whitened: float32 [2, 64, 1024, 512], P(None, 'gz', 'gx'), may hold values from -6 to 6
- observed: float32 [2, 1024, 512], P(None, 'gx'), may hold values from -12 to 12
- lower_x: bfloat16 [1024, 1024], P('gx'), as said below
- lower_y: bfloat16 [512, 512], P('gx'), as said below
- lower_z: bfloat16 [64, 64], replicated, as said below
- coupling_kernel: float32 [2, 3, 3, 3], replicated, may hold values from -1.25 to 1.25
Outputs:
- gradient: float32 [2, 64, 1024, 512], P(None, 'gz', 'gx')
- misfit: float32 [2, 1024, 512], P(None, 'gx')
Inputs may be any that keep to these rules, and one draw needn't show every extreme that they name: `lower_x`: lower triangular: zero above the diagonal, diagonal entries between 0.5 and 1.5. `lower_y`: lower triangular: zero above the diagonal, diagonal entries between 0.5 and 1.5. `lower_z`: lower triangular: zero above the diagonal, diagonal entries between 0.5 and 1.5.
All inputs are finite; a program needn't handle non-finite values.
Results may differ from a plain program's by a relative error of at most 0.013.
The roundings to bfloat16 on the way count: a program that leaves them out, or rounds other values in their place, can miss the bound.
Values may be sent and summed in bfloat16 or wider, within the bound.
A program may use at most 128 MiB of HBM per device.

v0:
```python
import math

import jax
import jax.numpy as jnp
from jax import lax
from jax.sharding import PartitionSpec as P

NZ = 64


def padded_2(x, sides, width):
    for axis, dim in sides:
        peers, length = (lax.axis_size(axis), x.shape[dim])
        up = [(i, (i + 1) % peers) for i in range(peers - 1)]
        down = [(j, i) for i, j in up]
        last = lax.slice_in_dim(x, length - width, length, axis=dim)
        first = lax.slice_in_dim(x, 0, width, axis=dim)
        before = lax.ppermute(last, axis, up)
        after = lax.ppermute(first, axis, down)
        x = jnp.concatenate([before, x, after], axis=dim)
    return x


def depth_lines(values, local_step):
    turned = lax.all_to_all(values, "gz", split_axis=3, concat_axis=1, tiled=True)
    return lax.all_to_all(local_step(turned), "gz", split_axis=1, concat_axis=3, tiled=True)


def across_lines(values, local_step):
    turned = lax.all_to_all(values, "gx", split_axis=3, concat_axis=2, tiled=True)
    return lax.all_to_all(local_step(turned), "gx", split_axis=2, concat_axis=3, tiled=True)


def stencil_sum(padded, kernel, depth_rows, x_rows, y_rows, flipped):
    total = jnp.zeros(padded.shape[:-3] + (depth_rows, x_rows, y_rows), jnp.float32)
    for offset_z in range(3):
        for offset_x in range(3):
            for offset_y in range(3):
                start_z = 2 - offset_z if flipped else offset_z
                start_x = 2 - offset_x if flipped else offset_x
                start_y = 2 - offset_y if flipped else offset_y
                total = (
                    total
                    + kernel[offset_z, offset_x, offset_y]
                    * padded[
                        ...,
                        start_z : start_z + depth_rows,
                        start_x : start_x + x_rows,
                        start_y : start_y + y_rows,
                    ]
                )
    return total


def depth_weights(first_row, depth_rows):
    depth = (first_row + jnp.arange(depth_rows)).astype(jnp.float32)
    factor = 4.0 / math.sqrt(NZ)
    return (factor / (1.0 + depth / NZ) ** 2, factor / (1.0 + depth / NZ) ** 3)


def coupling_forward(rim, magnetic_f, kernel, shape):
    depth_rows, x_rows, y_rows = shape
    pre_scale = stencil_sum(rim, kernel[0], depth_rows, x_rows, y_rows, False)
    pre_shift = stencil_sum(rim, kernel[1], depth_rows, x_rows, y_rows, False)
    scale = jnp.tanh(pre_scale)
    growth = jnp.exp(scale)
    return (scale, growth, magnetic_f * growth + pre_shift)


def local(whitened, observed, lower_x, lower_y, lower_z, coupling_kernel):
    factor_x, factor_y = (
        lax.all_gather(lower_x, "gx", axis=0, tiled=True),
        lax.all_gather(lower_y, "gx", axis=0, tiled=True),
    )

    def apply_depth(values):
        return jnp.einsum(
            "zk,fkxy->fzxy", lower_z, values, preferred_element_type=jnp.float32
        ).astype(jnp.bfloat16)

    def apply_across(values):
        return jnp.einsum(
            "xk,fzky->fzxy", factor_x, values, preferred_element_type=jnp.float32
        ).astype(jnp.bfloat16)

    def depth_adjoint(values):
        return jnp.einsum(
            "kz,fkxy->fzxy", lower_z, values, preferred_element_type=jnp.float32
        ).astype(jnp.bfloat16)

    def across_adjoint(values):
        return jnp.einsum(
            "kx,fzky->fzxy", factor_x, values, preferred_element_type=jnp.float32
        ).astype(jnp.bfloat16)

    start = whitened.astype(jnp.bfloat16)
    first = jnp.einsum("fzxk,yk->fzxy", start, factor_y, preferred_element_type=jnp.float32).astype(
        jnp.bfloat16
    )
    model = across_lines(depth_lines(first, apply_depth), apply_across)
    density = model[0]
    magnetic_f = model[1].astype(jnp.float32)
    depth_rows, x_rows, y_rows = density.shape
    rim = padded_2(density, (("gx", 1), ("gz", 0)), 1)
    rim = jnp.pad(rim, ((0, 0), (0, 0), (1, 1))).astype(jnp.float32)
    scale, growth, coupled = coupling_forward(
        rim, magnetic_f, coupling_kernel, (depth_rows, x_rows, y_rows)
    )
    weight_g, weight_m = depth_weights(lax.axis_index("gz") * depth_rows, depth_rows)
    part_g = jnp.einsum("z,zxy->xy", weight_g, density.astype(jnp.float32))
    part_m = jnp.einsum("z,zxy->xy", weight_m, coupled)
    predicted = lax.psum(jnp.stack([part_g, part_m]), "gz")
    misfit = predicted - observed
    back_g = weight_g[:, None, None] * misfit[0][None]
    back_m = weight_m[:, None, None] * misfit[1][None]
    back_scale = (back_m * magnetic_f * growth * (1.0 - scale * scale)).astype(jnp.bfloat16)
    back_shift = back_m.astype(jnp.bfloat16)
    cotangents = jnp.stack([back_scale, back_shift])
    outer = padded_2(cotangents, (("gx", 2), ("gz", 1)), 1)
    outer = jnp.pad(outer, ((0, 0), (0, 0), (0, 0), (1, 1))).astype(jnp.float32)
    spread_back = stencil_sum(outer[0], coupling_kernel[0], depth_rows, x_rows, y_rows, True)
    spread_back = spread_back + stencil_sum(
        outer[1], coupling_kernel[1], depth_rows, x_rows, y_rows, True
    )
    adjoint = jnp.stack([back_g + spread_back, back_m * growth]).astype(jnp.bfloat16)
    fourth = depth_lines(across_lines(adjoint, across_adjoint), depth_adjoint)
    gradient = whitened + jnp.einsum(
        "fzxk,ky->fzxy", fourth, factor_y, preferred_element_type=jnp.float32
    )
    return (gradient, misfit)


def solution(mesh):
    in_specs = (
        P(None, "gz", "gx", None),
        P(None, "gx", None),
        P("gx", None),
        P("gx", None),
        P(),
        P(),
    )
    out_specs = (P(None, "gz", "gx", None), P(None, "gx", None))
    return jax.shard_map(local, mesh=mesh, in_specs=in_specs, out_specs=out_specs, check_vma=False)
```

profile of v0, /device:TPU:0, one launch (start us, length us, event | category | flops | bytes accessed | tf_op | source)
XLA Modules:
  0.0 1368.1 jit_solution(581240853023325873)
XLA Ops:
  7.2 33.2 %all_gather.6 = bf16[512,512]{1,0:T(8,128)(2,1)S(1)} all-gather(bf16[64,512]{1,0:T(8,128)(2,1)} %param.9), channel_id=1, replica_groups=mesh['gx'=8,'gz'=4] {'gx'}, dimensions={0}, use_global_device_ids=true | all-gather | bytes 589824 | tf_op jit(solution)/shard_map/all_gather | solution.py:73
  41.2 7.8 fusion.77
  49.0 7.9 copy.51
  56.9 53.9 %all_to_all.141 = bf16[2,16,128,512]{2,1,0,3:T(8,128)(2,1)} all-to-all(bf16[2,16,128,512]{2,1,0,3:T(8,128)(2,1)} %copy.51), channel_id=1, replica_groups=mesh['gx'=8,'gz'=4] {'gz'}, dimensions={3} | all-to-all | bytes 8388608 | tf_op jit(solution)/shard_map/all_to_all | solution.py:25
  110.7 9.0 copy.52
  119.7 3.4 convert_bitcast_fusion.3
  123.1 2.7 copy.53
  125.8 51.6 %all_to_all.142 = bf16[2,64,128,128]{3,2,0,1:T(8,128)(2,1)} all-to-all(bf16[2,64,128,128]{3,2,0,1:T(8,128)(2,1)S(1)} %copy.53), channel_id=1, replica_groups=mesh['gx'=8,'gz'=4] {'gz'}, dimensions={1} | all-to-all | bytes 8388608 | tf_op jit(solution)/shard_map/all_to_all | solution.py:26
  177.4 7.8 copy.95
  185.3 5.7 all-to-all-start.2
  191.7 117.5 %all-to-all-done.2 = bf16[2,16,128,512]{2,1,0,3:T(8,128)(2,1)} async-done(((bf16[2,16,128,512]{2,1,0,3:T(8,128)(2,1)}), bf16[2,16,128,512]{2,1,0,3:T(8,128)(2,1)}, u32[]{:S(2)}, u32[]{:S(2)}) %all-to-all-start.2) | async-done | bytes 4194336 | tf_op jit(solution)/shard_map/all_to_all | solution.py:30
  309.2 6.9 copy.58
  316.1 7.3 all_to_all.113
  323.4 9.5 convert_bitcast_fusion.2
  332.8 12.9 copy.59
  345.7 10.5 reshape.38
  356.2 4.7 all-to-all-start.3
  363.3 90.1 %all-to-all-done.3 = bf16[8,2,131072]{2,1,0:T(2,128)(2,1)} async-done(((bf16[8,2,131072]{2,1,0:T(2,128)(2,1)}), bf16[8,2,131072]{2,1,0:T(2,128)(2,1)}, u32[]{:S(2)}, u32[]{:S(2)}) %all-to-all-start.3) | async-done | bytes 4194336 | tf_op jit(solution)/shard_map/all_to_all | solution.py:31
  453.4 10.3 reshape.39
  463.7 9.3 copy.97
  473.0 4.8 fusion.95
  478.4 2.8 fusion.96
  481.2 2.0 copy.63
  483.2 2.0 copy.64
  486.4 4.5 collective-permute-start
  491.7 3.0 copy.89
  494.7 1.8 copy.65
  496.5 1.8 copy.66
  503.2 2.8 copy.62
  506.6 11.4 fusion.10
  518.0 122.0 %add_add_fusion = (bf16[16,128,512]{1,2,0:T(8,128)(2,1)S(1)}, f32[16,128,512]{1,2,0:T(8,128)}) fusion(f32[16,128,512]{1,2,0:T(8,128)} %bitcast.166, f32[18,130,514]{1,2,0:T(8,128)} %fusion.10, f32[]{:T(128)} %bitcast.79, f32[]{:T(128)} %bitcast.78, f32[]{:T(128)} %bitcast.77, f32[]{:T(128)} %bitcast.76, f32[]{:T(128)} %bitcast.75, f32[]{:T(128)} %bitcast.74, ...), kind=kLoop, calls=%fused_computation.148 | loop fusion | flops 114294784 | bytes 123732184 | tf_op jit(solution)/shard_map/add | solution.py:67
  640.0 3.0 copy.91
  643.0 2.0 fusion.90
  645.9 35.0 %all-reduce.4.cloned.1.call-done = f32[2,128,512]{2,1,0:T(8,128)} async-done(((f32[2,128,512]{2,1,0:T(8,128)}), f32[2,128,512]{2,1,0:T(8,128)}) %all-reduce.4.cloned.1.call-update) | async-done | bytes 524304 | tf_op jit(solution)/shard_map/psum | solution.py:112
  683.5 6.4 fusion.81
  689.9 4.5 slice_maximum_fusion
  694.4 3.6 copy.70
  698.1 3.4 collective-permute-start.4
  701.5 3.8 copy.71
  706.6 3.2 copy.72
  711.1 3.2 copy.73
  714.3 2.9 pad_maximum_fusion.5
  720.2 3.2 collective-permute-done.7
  723.3 22.6 %fusion.1 = f32[2,18,130,514]{2,3,1,0:T(8,128)S(1)} fusion(bf16[2,1,130,512]{2,3,1,0:T(8,128)(2,1)} %collective-permute-done.7, bf16[2,1,130,512]{2,3,1,0:T(8,128)(2,1)S(1)} %collective-permute-done.6, bf16[2,16,1,512]{2,3,1,0:T(8,128)(2,1)} %copy.73, bf16[2,16,1,512]{2,3,1,0:T(8,128)(2,1)} %copy.72, bf16[1,16,128,512]{2,3,1,0:T(8,128)(2,1)S(1)} %multiply_convert_fusion, ...), kind=kLoop, calls=%fused_computation.8 | loop fusion | flops 50515920 | bytes 14414400 | tf_op jit(solution)/shard_map/convert_element_type | solution.py:120
  746.0 6.9 slice_bitcast_fusion.1
  752.9 196.9 %fusion.84 = bf16[1,16,128,512]{2,3,1,0:T(8,128)(2,1)S(1)} fusion(f32[18,130,514]{1,2,0:T(8,128)} %get-tuple-element.5, f32[]{:T(128)} %bitcast.79, f32[]{:T(128)} %bitcast.78, f32[]{:T(128)} %bitcast.77, f32[]{:T(128)} %bitcast.76, f32[]{:T(128)} %bitcast.75, f32[]{:T(128)} %bitcast.74, f32[]{:T(128)} %bitcast.73, f32[]{:T(128)} %bitcast.72, f32[]{:T(128)} %bitcast.71, ...), kind=kLoop, calls=%fused_computation.161 | loop fusion | flops 115343360 | bytes 228852000 | tf_op jit(solution)/shard_map/stack | solution.py:125
  950.2 2.7 copy.74
  952.9 97.5 %all_to_all.143 = bf16[2,16,128,512]{2,1,0,3:T(8,128)(2,1)S(1)} all-to-all(bf16[2,16,128,512]{2,1,0,3:T(8,128)(2,1)S(1)} %copy.74), channel_id=1, replica_groups=mesh['gx'=8,'gz'=4] {'gx'}, dimensions={3} | all-to-all | bytes 8388608 | tf_op jit(solution)/shard_map/all_to_all | solution.py:30
  1050.4 4.7 copy.76
  1055.1 7.4 all_to_all.120
  1062.6 8.4 convert_bitcast_fusion.1
  1070.9 12.9 copy.77
  1083.8 10.5 reshape.40
  1094.3 97.9 %all_to_all.144 = bf16[8,2,131072]{2,1,0:T(2,128)(2,1)} all-to-all(bf16[8,2,131072]{2,1,0:T(2,128)(2,1)} %reshape.40), channel_id=1, replica_groups=mesh['gx'=8,'gz'=4] {'gx'}, dimensions={0} | all-to-all | bytes 8388608 | tf_op jit(solution)/shard_map/all_to_all | solution.py:31
  1192.2 10.3 reshape.41
  1202.5 14.8 %copy.101 = bf16[2,16,128,8,64]{2,1,0,4,3:T(8,128)(2,1)} copy(bf16[2,16,128,8,64]{4,1,0,2,3:T(8,128)(2,1)} %bitcast.171) | data formatting | bytes 8388608 | tf_op jit(solution)/shard_map/all_to_all | solution.py:31
  1217.2 54.1 %all_to_all.145 = bf16[2,16,128,512]{2,1,0,3:T(8,128)(2,1)} all-to-all(bf16[2,16,128,512]{2,1,0,3:T(8,128)(2,1)} %bitcast.173), channel_id=1, replica_groups=mesh['gx'=8,'gz'=4] {'gz'}, dimensions={3} | all-to-all | bytes 8388608 | tf_op jit(solution)/shard_map/all_to_all | solution.py:25
  1271.3 9.0 copy.82
  1280.3 3.5 convert_bitcast_fusion
  1283.8 2.7 copy.84
  1286.5 50.7 %all_to_all.146 = bf16[2,64,128,128]{3,2,0,1:T(8,128)(2,1)S(1)} all-to-all(bf16[2,64,128,128]{3,2,0,1:T(8,128)(2,1)S(1)} %copy.84), channel_id=1, replica_groups=mesh['gx'=8,'gz'=4] {'gz'}, dimensions={1} | all-to-all | bytes 8388608 | tf_op jit(solution)/shard_map/all_to_all | solution.py:26
  1337.2 5.9 copy.109
  1343.2 7.2 all_to_all.132
  1350.4 10.4 convolution_add_fusion
  (63 shorter events, 21.2 us)
Async XLA Ops:
  7.2 112.5 %copy-start = (bf16[64,64]{1,0:T(8,128)(2,1)S(1)}, bf16[64,64]{1,0:T(8,128)(2,1)}, u32[]{:S(2)}) copy-start(bf16[64,64]{1,0:T(8,128)(2,1)} %param.10) | copy-start | bytes 24580
  40.4 0.8 copy-start.7
  185.3 123.9 %all-to-all-start.2 = ((bf16[2,16,128,512]{2,1,0,3:T(8,128)(2,1)}), bf16[2,16,128,512]{2,1,0,3:T(8,128)(2,1)}, u32[]{:S(2)}, u32[]{:S(2)}) async-start(bf16[2,16,128,512]{2,1,0,3:T(8,128)(2,1)} %bitcast.174), calls=%async_computation.2 | async-start | bytes 8388608 | tf_op jit(solution)/shard_map/all_to_all | solution.py:30
  191.0 132.4 %all-gather.2.cloned.1.call-start = ((), (), s32[]{:S(2)}) async-start(), calls=%async_computation.8 | async-start | bytes 2359296 | tf_op jit(solution)/shard_map/all_gather | solution.py:72
  356.2 5.0 copy-start.11
  356.2 97.2 %all-to-all-start.3 = ((bf16[8,2,131072]{2,1,0:T(2,128)(2,1)}), bf16[8,2,131072]{2,1,0:T(2,128)(2,1)}, u32[]{:S(2)}, u32[]{:S(2)}) async-start(bf16[8,2,131072]{2,1,0:T(2,128)(2,1)} %reshape.38), calls=%async_computation.3 | async-start | bytes 8388608 | tf_op jit(solution)/shard_map/all_to_all | solution.py:31
  360.9 320.0 %all-reduce.4.cloned.1.call-start = ((), (), s32[]{:S(2)}) async-start(), calls=%async_computation.9 | async-start | bytes 1048576 | tf_op jit(solution)/shard_map/psum | solution.py:112
  485.1 11.4 collective-permute-start.1
  486.4 8.3 collective-permute-start
  498.3 4.3 copy-start.5
  498.3 4.8 copy-start.4
  499.9 6.0 collective-permute-start.2
  501.4 4.6 collective-permute-start.3
  503.1 2.8 copy-start.2
  503.1 3.4 copy-start.3
  640.0 41.0 %copy-start.10 = (f32[2,128,512]{2,1,0:T(8,128)S(1)}, f32[2,128,512]{2,1,0:T(8,128)}, u32[]{:S(2)}) copy-start(f32[2,128,512]{2,1,0:T(8,128)} %param.7) | copy-start | bytes 1572868
  682.1 0.8 copy-start.9
  689.9 4.5 copy-start.1
  698.1 8.5 collective-permute-start.4
  705.3 5.8 collective-permute-start.5
  717.1 3.0 collective-permute-start.6
  718.5 4.9 collective-permute-start.7
  752.9 196.9 %copy-start.6 = (bf16[1,16,128,512]{2,3,1,0:T(8,128)(2,1)S(1)}, bf16[1,16,128,512]{2,3,1,0:T(8,128)(2,1)}, u32[]{:S(2)}) copy-start(bf16[1,16,128,512]{2,3,1,0:T(8,128)(2,1)} %get-tuple-element.11) | copy-start | bytes 6291460
  1055.1 7.4 copy-start.12
  1343.2 7.3 copy-start.8
Sparse Core Ops, SparseCore 0:
  193.9 102.6 all-gather.1
  646.0 34.8 all-reduce.3
where the time goes:
time: 1380 us; the launch traced here: 1370 us
  blocking collectives  439 us (32%)
  other arithmetic  376 us (27%)
  waiting for transfers between devices  248 us (18%)
  local copies, waits for them, and re-layouts  219 us (16%)
  matrix products  45.4 us (3%)
  starting transfers between devices  26.7 us (2%)
  between operations  14.8 us (1%)
    another operation x2, other arithmetic, local(): jnp.stack([back_g + spread_back, back_m * growth]).astype(jnp.bfloat16)  197 us
    add x1, other arithmetic, coupling_forward(): return (scale, growth, magnetic_f * growth + pre_shift)  122 us
    all_to_all x1, waiting for transfers between devices, across_lines(): lax.all_to_all(values, 'gx', split_axis=3, concat_axis=2, tiled=True)  117 us
    all_to_all x2, blocking collectives, depth_lines(): lax.all_to_all(values, 'gz', split_axis=3, concat_axis=1, tiled=True)  108 us
    all_to_all x2, blocking collectives, depth_lines(): lax.all_to_all(local_step(turned), 'gz', split_axis=1, concat_axis=3, til...  102 us
    all_to_all x1, blocking collectives, across_lines(): lax.all_to_all(local_step(turned), 'gx', split_axis=2, concat_axis=3, til...  97.9 us
    all_to_all x1, blocking collectives, across_lines(): lax.all_to_all(values, 'gx', split_axis=3, concat_axis=2, tiled=True)  97.5 us
    all_to_all x1, waiting for transfers between devices, across_lines(): lax.all_to_all(local_step(turned), 'gx', split_axis=2, concat_axis=3, til...  90.1 us
  transfers between devices with their start and end apart: 12, of which 6 were waited for; matrix products, arithmetic and copies ran while one was open for 2% of the time, Pallas kernels for 0%

commit v1 on v0

v1 whole, which is shorter than its diff:
```python
import math

import jax
import jax.numpy as jnp
from jax import lax
from jax.experimental import pallas as pl
from jax.experimental.pallas import tpu as pltpu
from jax.sharding import PartitionSpec as P

NZ = 64


def padded_2(x, sides, width):
    for axis, dim in sides:
        peers, length = (lax.axis_size(axis), x.shape[dim])
        up = [(i, (i + 1) % peers) for i in range(peers - 1)]
        down = [(j, i) for i, j in up]
        last = lax.slice_in_dim(x, length - width, length, axis=dim)
        first = lax.slice_in_dim(x, 0, width, axis=dim)
        before = lax.ppermute(last, axis, up)
        after = lax.ppermute(first, axis, down)
        x = jnp.concatenate([before, x, after], axis=dim)
    return x


def depth_lines(values, local_step):
    turned = lax.all_to_all(values, "gz", split_axis=2, concat_axis=1, tiled=True)
    return lax.all_to_all(local_step(turned), "gz", split_axis=1, concat_axis=2, tiled=True)


def across_lines(values, local_step):
    fields, depth, rows, cols = values.shape
    if (fields * depth) % lax.axis_size("gx"):
        turned = lax.all_to_all(values, "gx", split_axis=3, concat_axis=2, tiled=True)
        return lax.all_to_all(local_step(turned), "gx", split_axis=2, concat_axis=3, tiled=True)
    planes = values.reshape(1, fields * depth, rows, cols)
    turned = lax.all_to_all(planes, "gx", split_axis=1, concat_axis=2, tiled=True)
    back = lax.all_to_all(local_step(turned), "gx", split_axis=2, concat_axis=1, tiled=True)
    return back.reshape(values.shape)


CHUNK = 16
EDGE = 8


def edge_padded(rim):
    sides = ((EDGE - 1, EDGE - 1), (0, 0))
    return jnp.pad(rim, ((0, 0),) * (rim.ndim - 2) + sides).astype(jnp.float32)


def beside(low, high, middle):
    cols = middle.shape[1]
    lane = lax.broadcasted_iota(jnp.int32, middle.shape, 1)
    before = jnp.where(lane == 0, 0.0, pltpu.roll(low, 1, 1))
    after = jnp.where(lane == cols - 1, 0.0, pltpu.roll(high, cols - 1, 1))
    return middle + before + after


def forward_kernel(taps, weights, p0, p1, p2, magnetic, growth_out, slope_out, sums):
    z = pl.program_id(0)
    planes = (p0, p1, p2)
    weight_g, weight_m = weights[0, z], weights[1, z]

    @pl.when(z == 0)
    def _():
        sums[...] = jnp.zeros_like(sums)

    def part(row, mag):
        acc = [None] * 6
        for a in range(3):
            for b in range(3):
                at = row + EDGE - 1 + b
                v = planes[a][0, at : at + 8, :]
                for c in range(2):
                    for e in range(3):
                        term = taps[27 * c + 9 * a + 3 * b + e] * v
                        i = 3 * c + e
                        acc[i] = term if acc[i] is None else acc[i] + term
        scale = jnp.tanh(beside(acc[0], acc[2], acc[1]))
        shift = beside(acc[3], acc[5], acc[4])
        growth = jnp.exp(scale)
        out = slice(row, row + 8)
        growth_out[0, out, :] = growth
        slope_out[0, out, :] = mag * growth * (1.0 - scale * scale)
        density = p1[0, row + EDGE : row + EDGE + 8, :]
        sums[0, out, :] += weight_g * density
        sums[1, out, :] += weight_m * (mag * growth + shift)

    for row in range(0, magnetic.shape[1], CHUNK):
        mag = magnetic[0, row : row + CHUNK, :].astype(jnp.float32)
        part(row, mag[:8])
        part(row + 8, mag[8:])


def backward_kernel(taps, weights, p0, p1, p2, growth, misfit, out_ref):
    z = pl.program_id(0)
    planes = (p2, p1, p0)
    weight_g, weight_m = weights[0, z], weights[1, z]

    def part(row):
        acc = [None] * 3
        for c in range(2):
            for a in range(3):
                for b in range(3):
                    at = row + EDGE + 1 - b
                    v = planes[a][c, 0, at : at + 8, :]
                    for e in range(3):
                        term = taps[27 * c + 9 * a + 3 * b + e] * v
                        acc[e] = term if acc[e] is None else acc[e] + term
        spread = beside(acc[2], acc[0], acc[1])
        at = slice(row, row + 8)
        first = weight_g * misfit[0, at, :] + spread
        return first, weight_m * misfit[1, at, :] * growth[0, at, :]

    for row in range(0, growth.shape[1], CHUNK):
        d0, m0 = part(row)
        d1, m1 = part(row + 8)
        at = slice(row, row + CHUNK)
        out_ref[0, 0, at, :] = jnp.concatenate([d0, d1], 0).astype(jnp.bfloat16)
        out_ref[1, 0, at, :] = jnp.concatenate([m0, m1], 0).astype(jnp.bfloat16)


def params():
    return pltpu.CompilerParams(
        dimension_semantics=("arbitrary",), vmem_limit_bytes=40 * 1024 * 1024
    )


def cost(cells, flops, size):
    return pl.CostEstimate(flops=cells * flops, bytes_accessed=cells * size, transcendentals=0)


def coupling_forward(rim, magnetic, taps, weights):
    depth, rows, cols = magnetic.shape
    tall = rim.shape[1]
    smem = pl.BlockSpec(memory_space=pltpu.SMEM)
    plane = [pl.BlockSpec((1, tall, cols), lambda z, a=a: (z + a, 0, 0)) for a in range(3)]
    cells = pl.BlockSpec((1, rows, cols), lambda z: (z, 0, 0))
    full = jax.ShapeDtypeStruct(magnetic.shape, jnp.float32)
    return pl.pallas_call(
        forward_kernel,
        grid=(depth,),
        in_specs=[smem, smem, *plane, cells],
        out_specs=[cells, cells, pl.BlockSpec((2, rows, cols), lambda z: (0, 0, 0))],
        out_shape=[full, full, jax.ShapeDtypeStruct((2, rows, cols), jnp.float32)],
        compiler_params=params(),
        cost_estimate=cost(depth * rows * cols, 120, 24),
    )(taps, weights, rim, rim, rim, magnetic)


def coupling_backward(outer, growth, misfit, taps, weights):
    depth, rows, cols = growth.shape
    tall = outer.shape[2]
    smem = pl.BlockSpec(memory_space=pltpu.SMEM)
    plane = [pl.BlockSpec((2, 1, tall, cols), lambda z, a=a: (0, z + a, 0, 0)) for a in range(3)]
    return pl.pallas_call(
        backward_kernel,
        grid=(depth,),
        in_specs=[
            smem,
            smem,
            *plane,
            pl.BlockSpec((1, rows, cols), lambda z: (z, 0, 0)),
            pl.BlockSpec((2, rows, cols), lambda z: (0, 0, 0)),
        ],
        out_specs=pl.BlockSpec((2, 1, rows, cols), lambda z: (0, z, 0, 0)),
        out_shape=jax.ShapeDtypeStruct((2, depth, rows, cols), jnp.bfloat16),
        compiler_params=params(),
        cost_estimate=cost(depth * rows * cols, 120, 32),
    )(taps, weights, outer, outer, outer, growth, misfit)


def depth_weights(first_row, depth_rows):
    depth = (first_row + jnp.arange(depth_rows)).astype(jnp.float32)
    factor = 4.0 / math.sqrt(NZ)
    return (factor / (1.0 + depth / NZ) ** 2, factor / (1.0 + depth / NZ) ** 3)


def local(whitened, observed, lower_x, lower_y, lower_z, coupling_kernel):
    factor_x, factor_y = (
        lax.all_gather(lower_x, "gx", axis=0, tiled=True),
        lax.all_gather(lower_y, "gx", axis=0, tiled=True),
    )

    def apply_depth(values):
        return jnp.einsum(
            "zk,fkxy->fzxy", lower_z, values, preferred_element_type=jnp.float32
        ).astype(jnp.bfloat16)

    def apply_across(values):
        return jnp.einsum(
            "xk,fzky->fzxy", factor_x, values, preferred_element_type=jnp.float32
        ).astype(jnp.bfloat16)

    def depth_adjoint(values):
        return jnp.einsum(
            "kz,fkxy->fzxy", lower_z, values, preferred_element_type=jnp.float32
        ).astype(jnp.bfloat16)

    def across_adjoint(values):
        return jnp.einsum(
            "kx,fzky->fzxy", factor_x, values, preferred_element_type=jnp.float32
        ).astype(jnp.bfloat16)

    def apply_lines(values):
        first = jnp.einsum(
            "fzxk,yk->fzxy", values, factor_y, preferred_element_type=jnp.float32
        ).astype(jnp.bfloat16)
        return apply_depth(first)

    start = whitened.astype(jnp.bfloat16)
    model = across_lines(depth_lines(start, apply_lines), apply_across)
    density, magnetic = model[0], model[1]
    depth_rows = density.shape[0]
    taps = coupling_kernel.reshape(-1)
    weight_g, weight_m = depth_weights(lax.axis_index("gz") * depth_rows, depth_rows)
    weights = jnp.stack([weight_g, weight_m])
    rim = edge_padded(padded_2(density, (("gx", 1), ("gz", 0)), 1))
    growth, slope, sums = coupling_forward(rim, magnetic, taps, weights)
    misfit = lax.psum(sums, "gz") - observed
    back_m = weight_m[:, None, None] * misfit[1][None]
    cotangents = jnp.stack([back_m * slope, back_m]).astype(jnp.bfloat16)
    outer = edge_padded(padded_2(cotangents, (("gx", 2), ("gz", 1)), 1))
    adjoint = coupling_backward(outer, growth, misfit, taps, weights)
    fourth = depth_lines(across_lines(adjoint, across_adjoint), depth_adjoint)
    gradient = whitened + jnp.einsum(
        "fzxk,ky->fzxy", fourth, factor_y, preferred_element_type=jnp.float32
    )
    return (gradient, misfit)


def solution(mesh):
    in_specs = (
        P(None, "gz", "gx", None),
        P(None, "gx", None),
        P("gx", None),
        P("gx", None),
        P(),
        P(),
    )
    out_specs = (P(None, "gz", "gx", None), P(None, "gx", None))
    return jax.shard_map(local, mesh=mesh, in_specs=in_specs, out_specs=out_specs, check_vma=False)
```

time: 1380 us -> 932 us (0.68)
  other arithmetic: 376 us -> 12.8 us
  local copies, waits for them, and re-layouts: 219 us -> 85.8 us
  Pallas kernels: 0 us -> 89.8 us
  waiting for transfers between devices: 248 us -> 182 us
  blocking collectives: 439 us -> 480 us
    another operation x5 -> x3, other arithmetic: 209 us -> 1.24 us  [the longest x1 0.7 us: local(): cotangents = jnp.stack([back_m * slope, back_m]).astype(jnp.bfloat16)]
    add x1 -> x0, other arithmetic: 122 us -> none  [coupling_forward(): return (scale, growth, magnetic_f * growth + pre_shift)]
    pallas_call x0 -> x2, Pallas kernels: none -> 89.8 us  [the longest x1 47.2 us: coupling_forward(): pl.pallas_call(forward_kernel, grid=(depth,), in_specs=[smem, smem, *plan...]
    all_to_all x2, waiting for transfers between devices: 208 us -> 133 us  [the longest x1 117 us: across_lines(): lax.all_to_all(planes, 'gx', split_axis=1, concat_axis=2, tiled=True)]
    all_to_all x11 -> x9, local copies, waits for them, and re-layouts: 89.4 us -> 27.9 us  [the longest x2 15.1 us: across_lines(): lax.all_to_all(planes, 'gx', split_axis=1, concat_axis=2, tiled=True)]
    all_to_all x6, blocking collectives: 406 us -> 446 us  [the longest x2 196 us: across_lines(): lax.all_to_all(local_step(turned), 'gx', split_axis=2, concat_axis=1, til...]
    unnamed x31 -> x28, local copies, waits for them, and re-layouts: 43.8 us -> 17.6 us
    convert_element_type x3 -> x2, other arithmetic: 34.6 us -> 8.92 us  [edge_padded(): return jnp.pad(rim, ((0, 0),) * (rim.ndim - 2) + sides).astype(jnp.float32)]
  transfers between devices with their start and end apart: 12 -> 12, of which waited for: 6 -> 9; matrix products, arithmetic and copies ran while one was open for 2% -> 2% of each run, Pallas kernels for 0% -> 0%
where the time goes in v1:
time: 932 us; the launch traced here: 926 us
  blocking collectives  480 us (52%)
  waiting for transfers between devices  182 us (20%)
  Pallas kernels  89.8 us (10%)
  local copies, waits for them, and re-layouts  85.8 us (9%)
  matrix products  33.7 us (4%)
  starting transfers between devices  27.1 us (3%)
  between operations  14.5 us (2%)
  other arithmetic  12.8 us (1%)
    all_to_all x2, blocking collectives, across_lines(): lax.all_to_all(local_step(turned), 'gx', split_axis=2, concat_axis=1, til...  196 us
    all_to_all x1, waiting for transfers between devices, across_lines(): lax.all_to_all(planes, 'gx', split_axis=1, concat_axis=2, tiled=True)  117 us
    all_to_all x2, blocking collectives, depth_lines(): lax.all_to_all(local_step(turned), 'gz', split_axis=1, concat_axis=2, til...  102 us
    all_to_all x1, blocking collectives, across_lines(): lax.all_to_all(planes, 'gx', split_axis=1, concat_axis=2, tiled=True)  98 us
    all_to_all x1, blocking collectives, depth_lines(): lax.all_to_all(values, 'gz', split_axis=2, concat_axis=1, tiled=True)  50.9 us
    pallas_call x1, Pallas kernels, coupling_forward(): pl.pallas_call(forward_kernel, grid=(depth,), in_specs=[smem, smem, *plan...  47.2 us
    pallas_call x1, Pallas kernels, coupling_backward(): pl.pallas_call(backward_kernel, grid=(depth,), in_specs=[smem, smem, *pla...  42.6 us
    psum x1, waiting for transfers between devices, local(): misfit = lax.psum(sums, 'gz') - observed  34.4 us
  transfers between devices with their start and end apart: 12, of which 9 were waited for; matrix products, arithmetic and copies ran while one was open for 2% of the time, Pallas kernels for 0%

profile of v1, /device:TPU:0, one launch (start us, length us, event | category | flops | bytes accessed | tf_op | source)
XLA Modules:
  0.0 925.7 jit_solution(4382653359346491285)
XLA Ops:
  7.2 9.9 %copy.92 = bf16[2,16,128,512]{3,1,0,2:T(8,128)(2,1)} copy(f32[2,16,128,512]{3,2,1,0:T(8,128)} %param.6) | data formatting | bytes 12582912 | tf_op args[0]
  17.0 5.0 all-to-all-start
  22.0 33.5 %all_gather.6 = bf16[512,512]{1,0:T(8,128)(2,1)S(1)} all-gather(bf16[64,512]{1,0:T(8,128)(2,1)S(1)} %copy-done.8), channel_id=1, replica_groups=mesh['gx'=8,'gz'=4] {'gx'}, dimensions={0}, use_global_device_ids=true | all-gather | bytes 589824 | tf_op jit(solution)/shard_map/all_gather | solution.py:182
  55.6 15.3 %all-to-all-done = bf16[2,16,128,512]{3,1,0,2:T(8,128)(2,1)} async-done(((bf16[2,16,128,512]{3,1,0,2:T(8,128)(2,1)}), bf16[2,16,128,512]{3,1,0,2:T(8,128)(2,1)}, u32[]{:S(2)}, u32[]{:S(2)}) %all-to-all-start) | async-done | bytes 4194336 | tf_op jit(solution)/shard_map/all_to_all | solution.py:27
  70.9 6.7 copy.55
  77.6 8.8 convert_bitcast_fusion.3
  86.4 4.5 copy.57
  90.9 50.7 %all_to_all.129 = bf16[2,64,32,512]{3,2,0,1:T(8,128)(2,1)S(1)} all-to-all(bf16[2,64,32,512]{3,2,0,1:T(8,128)(2,1)S(1)} %copy.57), channel_id=1, replica_groups=mesh['gx'=8,'gz'=4] {'gz'}, dimensions={1} | all-to-all | bytes 8388608 | tf_op jit(solution)/shard_map/all_to_all | solution.py:28
  141.7 2.5 copy.59
  144.2 6.7 all-to-all-start.2
  150.9 0.7 all-gather.2.cloned.1.call-update
  151.6 0.3 all-reduce.4.cloned.1.call-start
  151.8 117.2 %all-to-all-done.2 = bf16[1,32,128,512]{3,2,0,1:T(8,128)(2,1)} async-done(((bf16[1,32,128,512]{3,2,0,1:T(8,128)(2,1)}), bf16[1,32,128,512]{3,2,0,1:T(8,128)(2,1)}, u32[]{:S(2)}, u32[]{:S(2)}) %all-to-all-start.2) | async-done | bytes 4194336 | tf_op jit(solution)/shard_map/all_to_all | solution.py:37
  269.0 7.6 copy.61
  276.6 7.3 reshape.80
  283.9 9.4 %convert_bitcast_fusion.2 = bf16[1,4,1024,512]{2,3,1,0:T(8,128)(2,1)} fusion(bf16[4,1024,512]{1,2,0:T(8,128)(2,1)} %reshape.80, bf16[1024,1024]{1,0:T(8,128)(2,1)} %all-gather.2.cloned.1.call-done), kind=kOutput, calls=%fused_computation.24 | convolution fusion | flops 4297064448 | bytes 10485760 | tf_op jit(solution)/shard_map/xk,fzky->fzxy/dot_general | solution.py:191
  293.3 7.8 copy.62
  301.2 96.9 %all_to_all.130 = bf16[1,4,1024,512]{3,1,0,2:T(4,128)(2,1)S(1)} all-to-all(bf16[1,4,1024,512]{3,1,0,2:T(4,128)(2,1)} %copy.62), channel_id=1, replica_groups=mesh['gx'=8,'gz'=4] {'gx'}, dimensions={2} | all-to-all | bytes 8388608 | tf_op jit(solution)/shard_map/all_to_all | solution.py:38
  398.1 1.1 copy.93
  399.2 0.3 fusion.38
  399.6 1.3 copy-done.6
  401.0 3.4 collective-permute-start
  404.3 1.3 collective-permute-start.1
  405.6 0.3 collective-permute-done
  405.9 4.2 collective-permute-done.1
  410.1 1.0 pad_maximum_fusion.6
  411.2 1.3 collective-permute-start.2
  412.5 1.3 collective-permute-start.3
  414.0 2.8 collective-permute-done.3
  416.8 4.0 fusion.22.p0.p1.p2
  420.8 47.2 %shard_map.77 = (f32[16,128,512]{2,1,0:T(8,128)S(1)}, f32[16,128,512]{2,1,0:T(8,128)S(1)}, f32[2,128,512]{2,1,0:T(8,128)}) custom-call(f32[54]{0:T(128)S(1)} %reshape.78.taps, f32[2,16]{1,0:T(2,128)S(1)} %pad_maximum_fusion.9.weights, f32[18,144,512]{2,1,0:T(8,128)} %fusion.22.p0.p1.p2, f32[18,144,512]{2,1,0:T(8,128)} %fusion.22.p0.p1.p2, ...), custom_call_target="tpu_custom_call" | custom-call | flops 125829120 | bytes 25165824 | tf_op jit(solution)/shard_map/pallas_call | solution.py:140
  468.0 2.0 copy-done.1
  470.0 2.0 copy-done.3
  472.1 34.4 %all-reduce.4.cloned.1.call-done = f32[2,128,512]{2,1,0:T(8,128)} async-done(((f32[2,128,512]{2,1,0:T(8,128)}), f32[2,128,512]{2,1,0:T(8,128)}) %all-reduce.4.cloned.1.call-update) | async-done | bytes 524304 | tf_op jit(solution)/shard_map/psum | solution.py:220
  506.5 1.3 sub.3.misfit
  507.8 0.5 multiply_convert_fusion
  508.3 0.7 copy-done.4
  509.0 0.7 fusion.28
  509.8 3.4 collective-permute-start.4
  513.2 1.7 collective-permute-start.5
  514.9 0.2 collective-permute-done.4
  515.1 4.3 collective-permute-done.5
  519.5 1.3 collective-permute-start.6
  520.9 1.6 collective-permute-start.7
  522.4 2.9 collective-permute-done.7
  525.3 4.9 fusion.1.p0.p1.p2
  530.2 42.6 %shard_map.78 = bf16[2,16,128,512]{3,2,1,0:T(8,128)(2,1)S(1)} custom-call(f32[54]{0:T(128)S(1)} %reshape.78.taps, f32[2,16]{1,0:T(2,128)S(1)} %pad_maximum_fusion.9.weights, f32[2,18,144,512]{3,2,1,0:T(8,128)} %fusion.1.p0.p1.p2, f32[2,18,144,512]{3,2,1,0:T(8,128)} %fusion.1.p0.p1.p2, f32[2,18,144,512]{3,2,1,0:T(8,128)} %fusion.1.p0.p1.p2, ...), custom_call_target="tpu_custom_call" | custom-call | flops 125829120 | bytes 33554432 | tf_op jit(solution)/shard_map/pallas_call | solution.py:156
  572.8 98.0 %all_to_all.131 = bf16[1,32,128,512]{3,2,0,1:T(8,128)(2,1)} all-to-all(bf16[1,32,128,512]{3,2,0,1:T(8,128)(2,1)S(1)} %bitcast.85), channel_id=1, replica_groups=mesh['gx'=8,'gz'=4] {'gx'}, dimensions={1} | all-to-all | bytes 8388608 | tf_op jit(solution)/shard_map/all_to_all | solution.py:37
  670.8 7.6 copy.65
  678.4 7.4 reshape.82
  685.8 8.2 convert_bitcast_fusion.1
  694.1 7.8 copy.66
  701.9 98.7 %all_to_all.132 = bf16[1,4,1024,512]{3,1,0,2:T(4,128)(2,1)S(1)} all-to-all(bf16[1,4,1024,512]{3,1,0,2:T(4,128)(2,1)} %copy.66), channel_id=1, replica_groups=mesh['gx'=8,'gz'=4] {'gx'}, dimensions={2} | all-to-all | bytes 8388608 | tf_op jit(solution)/shard_map/all_to_all | solution.py:38
  800.6 0.8 copy.67
  801.5 0.4 copy.68
  801.9 2.4 copy.69
  804.3 50.9 %all_to_all.133 = bf16[2,16,128,512]{3,1,0,2:T(8,128)(2,1)S(1)} all-to-all(bf16[2,16,128,512]{3,1,0,2:T(8,128)(2,1)S(1)} %copy.69), channel_id=1, replica_groups=mesh['gx'=8,'gz'=4] {'gz'}, dimensions={2} | all-to-all | bytes 8388608 | tf_op jit(solution)/shard_map/all_to_all | solution.py:27
  855.2 0.6 copy.71
  855.9 1.3 convert_bitcast_fusion
  857.2 2.4 copy.73
  859.6 51.0 %all_to_all.134 = bf16[2,64,32,512]{3,2,0,1:T(8,128)(2,1)S(1)} all-to-all(bf16[2,64,32,512]{3,2,0,1:T(8,128)(2,1)S(1)} %copy.73), channel_id=1, replica_groups=mesh['gx'=8,'gz'=4] {'gz'}, dimensions={1} | all-to-all | bytes 8388608 | tf_op jit(solution)/shard_map/all_to_all | solution.py:28
  910.6 0.6 copy.74
  911.2 1.6 slice-done.1
  912.8 5.9 convolution_add_fusion
  (36 shorter events, 0.6 us)
Async XLA Ops:
  7.2 70.4 %copy-start = (bf16[64,64]{1,0:T(8,128)(2,1)S(1)}, bf16[64,64]{1,0:T(8,128)(2,1)}, u32[]{:S(2)}) copy-start(bf16[64,64]{1,0:T(8,128)(2,1)} %param.10) | copy-start | bytes 24580
  17.0 5.0 copy-start.8
  17.0 53.8 %all-to-all-start = ((bf16[2,16,128,512]{3,1,0,2:T(8,128)(2,1)}), bf16[2,16,128,512]{3,1,0,2:T(8,128)(2,1)}, u32[]{:S(2)}, u32[]{:S(2)}) async-start(bf16[2,16,128,512]{3,1,0,2:T(8,128)(2,1)} %copy.92), calls=%async_computation | async-start | bytes 8388608 | tf_op jit(solution)/shard_map/all_to_all | solution.py:27
  144.2 124.9 %all-to-all-start.2 = ((bf16[1,32,128,512]{3,2,0,1:T(8,128)(2,1)}), bf16[1,32,128,512]{3,2,0,1:T(8,128)(2,1)}, u32[]{:S(2)}, u32[]{:S(2)}) async-start(bf16[1,32,128,512]{3,2,0,1:T(8,128)(2,1)} %bitcast.92), calls=%async_computation.2 | async-start | bytes 8388608 | tf_op jit(solution)/shard_map/all_to_all | solution.py:37
  150.8 133.1 %all-gather.2.cloned.1.call-start = ((), (), s32[]{:S(2)}) async-start(), calls=%async_computation.8 | async-start | bytes 2359296 | tf_op jit(solution)/shard_map/all_gather | solution.py:181
  151.6 354.9 %all-reduce.4.cloned.1.call-start = ((), (), s32[]{:S(2)}) async-start(), calls=%async_computation.9 | async-start | bytes 1048576 | tf_op jit(solution)/shard_map/psum | solution.py:220
  399.2 14.6 %copy-start.9 = (f32[2,3,3,3]{3,0,2,1:T(2,128)S(1)}, f32[2,3,3,3]{3,0,2,1:T(2,128)}, u32[]{:S(2)}) copy-start(f32[2,3,3,3]{3,0,2,1:T(2,128)} %param.11) | copy-start | bytes 652
  399.5 1.4 copy-start.6
  401.0 5.0 collective-permute-start
  404.3 5.8 collective-permute-start.1
  411.2 2.8 collective-permute-start.2
  412.5 4.3 collective-permute-start.3
  420.8 85.7 %copy-start.7 = (f32[2,128,512]{2,1,0:T(8,128)S(1)}, f32[2,128,512]{2,1,0:T(8,128)}, u32[]{:S(2)}) copy-start(f32[2,128,512]{2,1,0:T(8,128)} %param.7) | copy-start | bytes 1572868
  468.0 2.0 copy-start.1
  470.0 2.0 copy-start.3
  506.5 2.5 copy-start.4
  507.8 22.4 %copy-start.5 = (f32[2,128,512]{2,1,0:T(8,128)}, f32[2,128,512]{2,1,0:T(8,128)S(1)}, u32[]{:S(2)}) copy-start(f32[2,128,512]{2,1,0:T(8,128)S(1)} %sub.3.misfit) | copy-start | bytes 1572868
  509.8 5.3 collective-permute-start.4
  513.2 6.2 collective-permute-start.5
  519.5 2.9 collective-permute-start.6
  520.9 9.3 %copy-start.2 = (f32[16,128,512]{2,1,0:T(8,128)S(1)}, f32[16,128,512]{2,1,0:T(8,128)}, u32[]{:S(2)}) copy-start(f32[16,128,512]{2,1,0:T(8,128)} %copy-done.1) | copy-start | bytes 12582916
  520.9 4.4 collective-permute-start.7
  678.4 7.4 copy-start.10
  859.6 51.6 %slice-start = ((s8[8388608]{0:T(1024)(128)(4,1)}), s8[4194304]{0:T(1024)(128)(4,1)S(1)}, s32[]{:S(2)}) async-start(s8[8388608]{0:T(1024)(128)(4,1)} %bitcast.87), calls=%async_computation.10 | async-start | bytes 8388608
  910.6 2.2 slice-start.1
Sparse Core Ops, SparseCore 0:
  153.8 102.6 all-gather.1
  472.2 34.2 all-reduce.3

commit v2 on v1

v2 whole, which is shorter than its diff:
```python
import math

import jax
import jax.numpy as jnp
from jax import lax
from jax.experimental import pallas as pl
from jax.experimental.pallas import tpu as pltpu
from jax.sharding import PartitionSpec as P

NZ = 64


def padded_2(x, sides, width):
    for axis, dim in sides:
        peers, length = (lax.axis_size(axis), x.shape[dim])
        up = [(i, (i + 1) % peers) for i in range(peers - 1)]
        down = [(j, i) for i, j in up]
        last = lax.slice_in_dim(x, length - width, length, axis=dim)
        first = lax.slice_in_dim(x, 0, width, axis=dim)
        before = lax.ppermute(last, axis, up)
        after = lax.ppermute(first, axis, down)
        x = jnp.concatenate([before, x, after], axis=dim)
    return x


def moved(values, axis, split, concat):
    return lax.all_to_all(values, axis, split_axis=split, concat_axis=concat, tiled=True)


def total(values, axis):
    peers = lax.axis_size(axis)
    if peers & (peers - 1):
        return lax.psum(values, axis)
    step = 1
    while step < peers:
        values = values + lax.ppermute(values, axis, [(i, i ^ step) for i in range(peers)])
        step *= 2
    return values


def depth_lines(values, local_step):
    return moved(local_step(moved(values, "gz", 2, 1)), "gz", 1, 2)


def across_lines(values, local_step):
    if values.shape[1] % lax.axis_size("gx"):
        return moved(local_step(moved(values, "gx", 3, 2)), "gx", 2, 3)
    return moved(local_step(moved(values, "gx", 1, 2)), "gx", 2, 1)


CHUNK = 16
EDGE = 8


def edge_padded(rim):
    sides = ((EDGE - 1, EDGE - 1), (0, 0))
    return jnp.pad(rim, ((0, 0),) * (rim.ndim - 2) + sides).astype(jnp.float32)


def beside(low, high, middle):
    cols = middle.shape[1]
    lane = lax.broadcasted_iota(jnp.int32, middle.shape, 1)
    before = jnp.where(lane == 0, 0.0, pltpu.roll(low, 1, 1))
    after = jnp.where(lane == cols - 1, 0.0, pltpu.roll(high, cols - 1, 1))
    return middle + before + after


def forward_kernel(taps, weights, p0, p1, p2, growth_out, slope_out, sums):
    z = pl.program_id(0)
    planes = (p0, p1, p2)
    weight_g, weight_m = weights[0, z], weights[1, z]

    @pl.when(z == 0)
    def _():
        sums[...] = jnp.zeros_like(sums)

    for row in range(0, growth_out.shape[1], 8):
        acc = [None] * 6
        for a in range(3):
            for b in range(3):
                at = row + EDGE - 1 + b
                v = planes[a][0, at : at + 8, :]
                for c in range(2):
                    for e in range(3):
                        term = taps[27 * c + 9 * a + 3 * b + e] * v
                        i = 3 * c + e
                        acc[i] = term if acc[i] is None else acc[i] + term
        scale = jnp.tanh(beside(acc[0], acc[2], acc[1]))
        growth = jnp.exp(scale)
        out = slice(row, row + 8)
        growth_out[0, out, :] = growth
        slope_out[0, out, :] = growth * (1.0 - scale * scale)
        sums[0, out, :] += weight_g * p1[0, row + EDGE : row + EDGE + 8, :]
        sums[1, out, :] += weight_m * beside(acc[3], acc[5], acc[4])


def backward_kernel(taps, weights, p0, p1, p2, misfit, out_ref):
    z = pl.program_id(0)
    planes = (p2, p1, p0)

    def part(row):
        acc = [None] * 3
        for c in range(2):
            for a in range(3):
                for b in range(3):
                    at = row + EDGE + 1 - b
                    v = planes[a][c, 0, at : at + 8, :]
                    for e in range(3):
                        term = taps[27 * c + 9 * a + 3 * b + e] * v
                        acc[e] = term if acc[e] is None else acc[e] + term
        return weights[0, z] * misfit[row : row + 8, :] + beside(acc[2], acc[0], acc[1])

    for row in range(0, out_ref.shape[1], CHUNK):
        both = jnp.concatenate([part(row), part(row + 8)], 0)
        out_ref[0, row : row + CHUNK, :] = both.astype(jnp.bfloat16)


def params():
    return pltpu.CompilerParams(
        dimension_semantics=("arbitrary",), vmem_limit_bytes=40 * 1024 * 1024
    )


def cost(cells, flops, size):
    return pl.CostEstimate(flops=cells * flops, bytes_accessed=cells * size, transcendentals=0)


def coupling_forward(rim, taps, weights):
    depth, tall, cols = rim.shape[0] - 2, rim.shape[1], rim.shape[2]
    rows = tall - 2 * EDGE
    smem = pl.BlockSpec(memory_space=pltpu.SMEM)
    plane = [pl.BlockSpec((1, tall, cols), lambda z, a=a: (z + a, 0, 0)) for a in range(3)]
    cells = pl.BlockSpec((1, rows, cols), lambda z: (z, 0, 0))
    full = jax.ShapeDtypeStruct((depth, rows, cols), jnp.float32)
    return pl.pallas_call(
        forward_kernel,
        grid=(depth,),
        in_specs=[smem, smem, *plane],
        out_specs=[cells, cells, pl.BlockSpec((2, rows, cols), lambda z: (0, 0, 0))],
        out_shape=[full, full, jax.ShapeDtypeStruct((2, rows, cols), jnp.float32)],
        compiler_params=params(),
        cost_estimate=cost(depth * rows * cols, 1200, 24),
    )(taps, weights, rim, rim, rim)


def coupling_backward(outer, misfit, taps, weights):
    depth, tall, cols = outer.shape[1] - 2, outer.shape[2], outer.shape[3]
    rows = tall - 2 * EDGE
    smem = pl.BlockSpec(memory_space=pltpu.SMEM)
    plane = [pl.BlockSpec((2, 1, tall, cols), lambda z, a=a: (0, z + a, 0, 0)) for a in range(3)]
    return pl.pallas_call(
        backward_kernel,
        grid=(depth,),
        in_specs=[
            smem,
            smem,
            *plane,
            pl.BlockSpec((rows, cols), lambda z: (0, 0)),
        ],
        out_specs=pl.BlockSpec((1, rows, cols), lambda z: (z, 0, 0)),
        out_shape=jax.ShapeDtypeStruct((depth, rows, cols), jnp.bfloat16),
        compiler_params=params(),
        cost_estimate=cost(depth * rows * cols, 1200, 32),
    )(taps, weights, outer, outer, outer, misfit)


def depth_weights(first_row, depth_rows):
    depth = (first_row + jnp.arange(depth_rows)).astype(jnp.float32)
    factor = 4.0 / math.sqrt(NZ)
    return (factor / (1.0 + depth / NZ) ** 2, factor / (1.0 + depth / NZ) ** 3)


def local(whitened, observed, lower_x, lower_y, lower_z, coupling_kernel):
    factor_x, factor_y = (
        lax.all_gather(lower_x, "gx", axis=0, tiled=True),
        lax.all_gather(lower_y, "gx", axis=0, tiled=True),
    )

    def apply_depth(values):
        return jnp.einsum(
            "zk,fkxy->fzxy", lower_z, values, preferred_element_type=jnp.float32
        ).astype(jnp.bfloat16)

    def apply_across(values):
        return jnp.einsum(
            "xk,fzky->fzxy", factor_x, values, preferred_element_type=jnp.float32
        ).astype(jnp.bfloat16)

    def depth_adjoint(values):
        return jnp.einsum(
            "kz,fkxy->fzxy", lower_z, values, preferred_element_type=jnp.float32
        ).astype(jnp.bfloat16)

    def across_adjoint(values):
        return jnp.einsum(
            "kx,fzky->fzxy", factor_x, values, preferred_element_type=jnp.float32
        ).astype(jnp.bfloat16)

    def apply_lines(values):
        first = jnp.einsum(
            "fzxk,yk->fzxy", values, factor_y, preferred_element_type=jnp.float32
        ).astype(jnp.bfloat16)
        return apply_depth(first)

    start = whitened.astype(jnp.bfloat16)
    def to_model(field):
        return across_lines(depth_lines(start[field : field + 1], apply_lines), apply_across)[0]

    def to_gradient(field, adjoint):
        fourth = depth_lines(across_lines(adjoint[None], across_adjoint), depth_adjoint)
        return whitened[field : field + 1] + jnp.einsum(
            "fzxk,ky->fzxy", fourth, factor_y, preferred_element_type=jnp.float32
        )

    density = to_model(0)
    magnetic = to_model(1).astype(jnp.float32)
    depth_rows = density.shape[0]
    taps = coupling_kernel.reshape(-1)
    weight_g, weight_m = depth_weights(lax.axis_index("gz") * depth_rows, depth_rows)
    weights = jnp.stack([weight_g, weight_m])
    rim = edge_padded(padded_2(density, (("gx", 1), ("gz", 0)), 1))
    growth, slope, sums = coupling_forward(rim, taps, weights)
    part_m = sums[1] + jnp.sum(weight_m[:, None, None] * (magnetic * growth), axis=0)
    misfit_g = total(sums[0], "gz") - observed[0]
    misfit_m = total(part_m, "gz") - observed[1]
    back_m = weight_m[:, None, None] * misfit_m[None]
    gradient_m = to_gradient(1, (back_m * growth).astype(jnp.bfloat16))
    cotangents = jnp.stack([back_m * magnetic * slope, back_m]).astype(jnp.bfloat16)
    outer = edge_padded(padded_2(cotangents, (("gx", 2), ("gz", 1)), 1))
    gradient_g = to_gradient(0, coupling_backward(outer, misfit_g, taps, weights))
    return (jnp.concatenate([gradient_g, gradient_m]), jnp.stack([misfit_g, misfit_m]))


def solution(mesh):
    in_specs = (
        P(None, "gz", "gx", None),
        P(None, "gx", None),
        P("gx", None),
        P("gx", None),
        P(),
        P(),
    )
    out_specs = (P(None, "gz", "gx", None), P(None, "gx", None))
    return jax.shard_map(local, mesh=mesh, in_specs=in_specs, out_specs=out_specs, check_vma=False)
```

time: 932 us -> 876 us (0.940)
  blocking collectives: 480 us -> 62.1 us
  waiting for transfers between devices: 182 us -> 407 us
  starting transfers between devices: 27.1 us -> 116 us
  local copies, waits for them, and re-layouts: 85.8 us -> 121 us
  matrix products: 33.7 us -> 43.2 us
    all_to_all x6 -> x1, blocking collectives: 446 us -> 29.8 us  [moved(): lax.all_to_all(values, axis, split_axis=split, concat_axis=concat, tiled=...]
    all_to_all x2 -> x15, waiting for transfers between devices: 133 us -> 366 us  [moved(): lax.all_to_all(values, axis, split_axis=split, concat_axis=concat, tiled=...]
    all_to_all x2 -> x15, starting transfers between devices: 11.6 us -> 98.9 us  [moved(): lax.all_to_all(values, axis, split_axis=split, concat_axis=concat, tiled=...]
    psum x1 -> x0, waiting for transfers between devices: 34.4 us -> none  [local(): misfit = lax.psum(sums, 'gz') - observed]
    ppermute x4, waiting for transfers between devices: 0.46 us -> 23.6 us  [padded_2(): before = lax.ppermute(last, axis, up)]
    all_to_all x9 -> x23, local copies, waits for them, and re-layouts: 27.9 us -> 47.3 us  [moved(): lax.all_to_all(values, axis, split_axis=split, concat_axis=concat, tiled=...]
    ppermute x0 -> x4, waiting for transfers between devices: none -> 13.8 us  [total(): lax.ppermute(values, axis, [(i, i ^ step) for i in range(peers)])]
    ppermute x4, waiting for transfers between devices: 14.2 us -> 2.97 us  [padded_2(): after = lax.ppermute(first, axis, down)]
  transfers between devices with their start and end apart: 12 -> 28, of which waited for: 9 -> 20; matrix products, arithmetic and copies ran while one was open for 2% -> 17% of each run, Pallas kernels for 0% -> 5%
where the time goes in v2:
time: 876 us; the launch traced here: 866 us
  waiting for transfers between devices  407 us (46%)
  local copies, waits for them, and re-layouts  121 us (14%)
  starting transfers between devices  116 us (13%)
  Pallas kernels  88.4 us (10%)
  blocking collectives  62.1 us (7%)
  matrix products  43.2 us (5%)
  between operations  15 us (2%)
  other arithmetic  13.6 us (2%)
    all_to_all x15, waiting for transfers between devices, moved(): lax.all_to_all(values, axis, split_axis=split, concat_axis=concat, tiled=...  366 us
    all_to_all x15, starting transfers between devices, moved(): lax.all_to_all(values, axis, split_axis=split, concat_axis=concat, tiled=...  98.9 us
    all_to_all x23, local copies, waits for them, and re-layouts, moved(): lax.all_to_all(values, axis, split_axis=split, concat_axis=concat, tiled=...  47.3 us
    pallas_call x1, Pallas kernels, coupling_forward(): pl.pallas_call(forward_kernel, grid=(depth,), in_specs=[smem, smem, *plan...  45.2 us
    pallas_call x1, Pallas kernels, coupling_backward(): pl.pallas_call(backward_kernel, grid=(depth,), in_specs=[smem, smem, *pla...  43.2 us
    all_gather x1, blocking collectives, local(): lax.all_gather(lower_y, 'gx', axis=0, tiled=True)  32.3 us
    all_to_all x1, blocking collectives, moved(): lax.all_to_all(values, axis, split_axis=split, concat_axis=concat, tiled=...  29.8 us
    ppermute x4, waiting for transfers between devices, padded_2(): before = lax.ppermute(last, axis, up)  23.6 us
  transfers between devices with their start and end apart: 28, of which 20 were waited for; matrix products, arithmetic and copies ran while one was open for 17% of the time, Pallas kernels for 5%

profile of v2, /device:TPU:0, one launch (start us, length us, event | category | flops | bytes accessed | tf_op | source)
XLA Modules:
  0.0 865.7 jit_solution(5026730918687047339)
XLA Ops:
  7.2 7.8 copy.154
  16.8 29.8 %all_to_all.246 = bf16[1,16,128,512]{3,1,0,2:T(8,128)(2,1)} all-to-all(bf16[1,16,128,512]{3,1,0,2:T(8,128)(2,1)S(1)} %get-tuple-element.13), channel_id=1, replica_groups=mesh['gx'=8,'gz'=4] {'gz'}, dimensions={2} | all-to-all | bytes 4194304 | tf_op jit(solution)/shard_map/all_to_all | solution.py:27
  46.6 3.7 all-to-all-start.4
  50.3 32.3 %all_gather.6 = bf16[512,512]{1,0:T(8,128)(2,1)S(1)} all-gather(bf16[64,512]{1,0:T(8,128)(2,1)S(1)} %copy-done.10), channel_id=1, replica_groups=mesh['gx'=8,'gz'=4] {'gx'}, dimensions={0}, use_global_device_ids=true | all-gather | bytes 589824 | tf_op jit(solution)/shard_map/all_gather | solution.py:176
  87.0 5.2 convert_bitcast_fusion.7
  92.3 4.1 copy.96
  96.4 5.0 all-to-all-start.1
  102.8 3.6 convert_bitcast_fusion.5
  106.4 4.1 copy.105
  110.5 16.6 %all-to-all-done.1 = bf16[1,64,32,512]{3,2,0,1:T(8,128)(2,1)} async-done(((bf16[1,64,32,512]{3,2,0,1:T(8,128)(2,1)}), bf16[1,64,32,512]{3,2,0,1:T(8,128)(2,1)}, u32[]{:S(2)}, u32[]{:S(2)}) %all-to-all-start.1) | async-done | bytes 2097184 | tf_op jit(solution)/shard_map/all_to_all | solution.py:27
  127.1 3.6 all-to-all-start.5
  130.7 3.2 copy.97
  133.9 22.5 %all-to-all-done.5 = bf16[1,64,32,512]{3,2,0,1:T(8,128)(2,1)S(1)} async-done(((bf16[1,64,32,512]{3,2,0,1:T(8,128)(2,1)}), bf16[1,64,32,512]{3,2,0,1:T(8,128)(2,1)S(1)}, u32[]{:S(2)}, u32[]{:S(2)}) %all-to-all-start.5) | async-done | bytes 2097184 | tf_op jit(solution)/shard_map/all_to_all | solution.py:27
  156.4 5.5 all-to-all-start.2
  164.1 68.4 %all-to-all-done.2 = bf16[1,16,128,512]{3,2,0,1:T(8,128)(2,1)} async-done(((bf16[1,16,128,512]{3,2,0,1:T(8,128)(2,1)}), bf16[1,16,128,512]{3,2,0,1:T(8,128)(2,1)}, u32[]{:S(2)}, u32[]{:S(2)}) %all-to-all-start.2) | async-done | bytes 2097184 | tf_op jit(solution)/shard_map/all_to_all | solution.py:27
  232.5 3.6 all-to-all-start.6
  236.1 4.3 copy.99
  240.4 4.2 reshape.124
  244.6 5.9 convert_bitcast_fusion.6
  250.5 6.2 copy.100
  256.7 26.6 %all-to-all-done.6 = bf16[1,16,128,512]{3,2,0,1:T(8,128)(2,1)S(1)} async-done(((bf16[1,16,128,512]{3,2,0,1:T(8,128)(2,1)}), bf16[1,16,128,512]{3,2,0,1:T(8,128)(2,1)S(1)}, u32[]{:S(2)}, u32[]{:S(2)}) %all-to-all-start.6) | async-done | bytes 2097184 | tf_op jit(solution)/shard_map/all_to_all | solution.py:27
  284.6 3.6 all-to-all-start.3
  288.3 4.4 copy.108
  292.6 4.2 reshape.126
  296.8 6.0 convert_bitcast_fusion.4
  302.8 6.2 copy.109
  308.9 27.8 %all-to-all-done.3 = bf16[1,2,1024,512]{3,1,0,2:T(2,128)(2,1)S(1)} async-done(((bf16[1,2,1024,512]{3,1,0,2:T(2,128)(2,1)}), bf16[1,2,1024,512]{3,1,0,2:T(2,128)(2,1)S(1)}, u32[]{:S(2)}, u32[]{:S(2)}) %all-to-all-start.3) | async-done | bytes 2097184 | tf_op jit(solution)/shard_map/all_to_all | solution.py:27
  338.0 4.4 all-to-all-start.7
  344.5 3.8 collective-permute-start
  349.6 10.8 %collective-permute-done = bf16[16,1,512]{2,1,0:T(2,128)(2,1)S(1)} collective-permute-done((bf16[16,1,512]{2,1,0:T(2,128)(2,1)S(1)}, bf16[16,1,512]{2,1,0:T(2,128)(2,1)S(1)}, u32[]{:S(2)}, u32[]{:S(2)}) %collective-permute-start) | collective-permute-done | bytes 16416 | tf_op jit(solution)/shard_map/ppermute | solution.py:20
  363.4 27.1 %all-to-all-done.7 = bf16[1,2,1024,512]{3,1,0,2:T(2,128)(2,1)} async-done(((bf16[1,2,1024,512]{3,1,0,2:T(2,128)(2,1)}), bf16[1,2,1024,512]{3,1,0,2:T(2,128)(2,1)}, u32[]{:S(2)}, u32[]{:S(2)}) %all-to-all-start.7) | async-done | bytes 2097184 | tf_op jit(solution)/shard_map/all_to_all | solution.py:27
  393.7 45.2 %shard_map.77 = (f32[16,128,512]{2,1,0:T(8,128)S(1)}, f32[16,128,512]{2,1,0:T(8,128)S(1)}, f32[2,128,512]{2,1,0:T(8,128)S(1)}) custom-call(f32[54]{0:T(128)S(1)} %reshape.122.taps, f32[2,16]{1,0:T(2,128)S(1)} %pad_maximum_fusion.11.weights, f32[18,144,512]{2,1,0:T(8,128)S(1)} %fusion.15.p0.p1.p2, f32[18,144,512]{2,1,0:T(8,128)S(1)} %fusion.15.p0.p1.p2, ...), custom_call_target="tpu_custom_call" | custom-call | flops 1258291200 | bytes 25165824 | tf_op jit(solution)/shard_map/pallas_call | solution.py:135
  443.0 7.0 collective-permute-done.11
  450.0 5.0 collective-permute-done.5
  455.2 3.3 fusion.11
  458.5 8.7 %all-to-all-start.12 = ((bf16[1,16,128,512]{3,2,0,1:T(8,128)(2,1)}), bf16[1,16,128,512]{3,2,0,1:T(8,128)(2,1)}, u32[]{:S(2)}, u32[]{:S(2)}) async-start(bf16[1,16,128,512]{3,2,0,1:T(8,128)(2,1)} %get-tuple-element.23), calls=%async_computation.12 | async-start | bytes 4194304 | tf_op jit(solution)/shard_map/all_to_all | solution.py:27
  467.9 3.9 collective-permute-start.6
  473.1 12.7 %collective-permute-done.6 = bf16[2,16,1,512]{3,2,1,0:T(2,128)(2,1)S(1)} collective-permute-done((bf16[2,16,1,512]{3,2,1,0:T(2,128)(2,1)S(1)}, bf16[2,16,1,512]{3,2,1,0:T(2,128)(2,1)S(1)}, u32[]{:S(2)}, u32[]{:S(2)}) %collective-permute-start.6) | collective-permute-done | bytes 32800 | tf_op jit(solution)/shard_map/ppermute | solution.py:20
  493.4 43.2 %shard_map.78 = bf16[16,128,512]{2,1,0:T(8,128)(2,1)} custom-call(f32[54]{0:T(128)S(1)} %reshape.122.taps, f32[2,16]{1,0:T(2,128)S(1)} %pad_maximum_fusion.11.weights, f32[2,18,144,512]{3,2,1,0:T(8,128)S(1)} %fusion.1.p0.p1.p2, f32[2,18,144,512]{3,2,1,0:T(8,128)S(1)} %fusion.1.p0.p1.p2, f32[2,18,144,512]{3,2,1,0:T(8,128)S(1)} %fusion.1.p0.p1.p2, ...), custom_call_target="tpu_custom_call" | custom-call | flops 1258291200 | bytes 33554432 | tf_op jit(solution)/shard_map/pallas_call | solution.py:151
  536.6 34.4 %all-to-all-start.8 = ((bf16[1,16,128,512]{3,2,0,1:T(8,128)(2,1)}), bf16[1,16,128,512]{3,2,0,1:T(8,128)(2,1)S(1)}, u32[]{:S(2)}, u32[]{:S(2)}) async-start(bf16[1,16,128,512]{3,2,0,1:T(8,128)(2,1)} %bitcast.42), calls=%async_computation.8 | async-start | bytes 4194304 | tf_op jit(solution)/shard_map/all_to_all | solution.py:27
  571.0 4.3 copy.123
  575.4 4.2 reshape.130
  579.5 5.9 convert_bitcast_fusion.1
  585.4 6.2 copy.124
  591.6 26.4 %all-to-all-done.8 = bf16[1,16,128,512]{3,2,0,1:T(8,128)(2,1)S(1)} async-done(((bf16[1,16,128,512]{3,2,0,1:T(8,128)(2,1)}), bf16[1,16,128,512]{3,2,0,1:T(8,128)(2,1)S(1)}, u32[]{:S(2)}, u32[]{:S(2)}) %all-to-all-start.8) | async-done | bytes 2097184 | tf_op jit(solution)/shard_map/all_to_all | solution.py:27
  619.3 6.2 all-to-all-start.13
  625.4 4.4 copy.112
  629.8 4.2 reshape.127
  634.0 5.9 convert_bitcast_fusion.3
  639.9 6.2 copy.113
  646.0 28.4 %all-to-all-done.13 = bf16[1,2,1024,512]{3,1,0,2:T(2,128)(2,1)S(1)} async-done(((bf16[1,2,1024,512]{3,1,0,2:T(2,128)(2,1)}), bf16[1,2,1024,512]{3,1,0,2:T(2,128)(2,1)S(1)}, u32[]{:S(2)}, u32[]{:S(2)}) %all-to-all-start.13) | async-done | bytes 2097184 | tf_op jit(solution)/shard_map/all_to_all | solution.py:27
  674.5 4.4 all-to-all-start.9
  681.9 45.2 %all-to-all-done.9 = bf16[1,2,1024,512]{3,1,0,2:T(2,128)(2,1)} async-done(((bf16[1,2,1024,512]{3,1,0,2:T(2,128)(2,1)}), bf16[1,2,1024,512]{3,1,0,2:T(2,128)(2,1)}, u32[]{:S(2)}, u32[]{:S(2)}) %all-to-all-start.9) | async-done | bytes 2097184 | tf_op jit(solution)/shard_map/all_to_all | solution.py:27
  727.1 3.6 all-to-all-start.14
  735.3 21.0 %all-to-all-done.14 = bf16[1,16,128,512]{3,1,0,2:T(8,128)(2,1)S(1)} async-done(((bf16[1,16,128,512]{3,1,0,2:T(8,128)(2,1)}), bf16[1,16,128,512]{3,1,0,2:T(8,128)(2,1)S(1)}, u32[]{:S(2)}, u32[]{:S(2)}) %all-to-all-start.14) | async-done | bytes 2097184 | tf_op jit(solution)/shard_map/all_to_all | solution.py:27
  757.7 3.9 all-to-all-start.10
  768.7 18.5 %all-to-all-done.10 = bf16[1,16,128,512]{3,1,0,2:T(8,128)(2,1)S(1)} async-done(((bf16[1,16,128,512]{3,1,0,2:T(8,128)(2,1)}), bf16[1,16,128,512]{3,1,0,2:T(8,128)(2,1)S(1)}, u32[]{:S(2)}, u32[]{:S(2)}) %all-to-all-start.10) | async-done | bytes 2097184 | tf_op jit(solution)/shard_map/all_to_all | solution.py:27
  788.5 3.6 all-to-all-start.15
  799.4 18.4 %all-to-all-done.15 = bf16[1,64,32,512]{3,2,0,1:T(8,128)(2,1)S(1)} async-done(((bf16[1,64,32,512]{3,2,0,1:T(8,128)(2,1)}), bf16[1,64,32,512]{3,2,0,1:T(8,128)(2,1)S(1)}, u32[]{:S(2)}, u32[]{:S(2)}) %all-to-all-start.15) | async-done | bytes 2097184 | tf_op jit(solution)/shard_map/all_to_all | solution.py:27
  817.8 4.8 all-to-all-start.11
  823.7 5.5 bitcast_add_fusion
  829.1 19.2 %all-to-all-done.11 = bf16[1,64,32,512]{3,2,0,1:T(8,128)(2,1)} async-done(((bf16[1,64,32,512]{3,2,0,1:T(8,128)(2,1)}), bf16[1,64,32,512]{3,2,0,1:T(8,128)(2,1)}, u32[]{:S(2)}, u32[]{:S(2)}) %all-to-all-start.11) | async-done | bytes 2097184 | tf_op jit(solution)/shard_map/all_to_all | solution.py:27
  850.2 3.7 bitcast_add_fusion.1
  853.9 4.4 pad_maximum_fusion
  (89 shorter events, 64.4 us)
Async XLA Ops:
  7.2 79.9 %copy-start = (bf16[64,64]{1,0:T(8,128)(2,1)S(1)}, bf16[64,64]{1,0:T(8,128)(2,1)}, u32[]{:S(2)}) copy-start(bf16[64,64]{1,0:T(8,128)(2,1)} %param.10) | copy-start | bytes 24580
  46.6 3.8 copy-start.10
  46.6 49.8 %all-to-all-start.4 = ((bf16[1,16,128,512]{3,1,0,2:T(8,128)(2,1)}), bf16[1,16,128,512]{3,1,0,2:T(8,128)(2,1)S(1)}, u32[]{:S(2)}, u32[]{:S(2)}) async-start(bf16[1,16,128,512]{3,1,0,2:T(8,128)(2,1)} %get-tuple-element.12), calls=%async_computation.4 | async-start | bytes 4194304 | tf_op jit(solution)/shard_map/all_to_all | solution.py:27
  96.4 30.7 %all-to-all-start.1 = ((bf16[1,64,32,512]{3,2,0,1:T(8,128)(2,1)}), bf16[1,64,32,512]{3,2,0,1:T(8,128)(2,1)}, u32[]{:S(2)}, u32[]{:S(2)}) async-start(bf16[1,64,32,512]{3,2,0,1:T(8,128)(2,1)} %copy.96), calls=%async_computation.1 | async-start | bytes 4194304 | tf_op jit(solution)/shard_map/all_to_all | solution.py:27
  127.1 29.3 %all-to-all-start.5 = ((bf16[1,64,32,512]{3,2,0,1:T(8,128)(2,1)}), bf16[1,64,32,512]{3,2,0,1:T(8,128)(2,1)S(1)}, u32[]{:S(2)}, u32[]{:S(2)}) async-start(bf16[1,64,32,512]{3,2,0,1:T(8,128)(2,1)} %copy.105), calls=%async_computation.5 | async-start | bytes 4194304 | tf_op jit(solution)/shard_map/all_to_all | solution.py:27
  156.4 76.1 %all-to-all-start.2 = ((bf16[1,16,128,512]{3,2,0,1:T(8,128)(2,1)}), bf16[1,16,128,512]{3,2,0,1:T(8,128)(2,1)}, u32[]{:S(2)}, u32[]{:S(2)}) async-start(bf16[1,16,128,512]{3,2,0,1:T(8,128)(2,1)} %bitcast.201), calls=%async_computation.2 | async-start | bytes 4194304 | tf_op jit(solution)/shard_map/all_to_all | solution.py:27
  161.9 82.7 %all-gather.2.cloned.1.call-start = ((), (), s32[]{:S(2)}) async-start(), calls=%async_computation.16 | async-start | bytes 2359296 | tf_op jit(solution)/shard_map/all_gather | solution.py:175
  232.5 50.8 %all-to-all-start.6 = ((bf16[1,16,128,512]{3,2,0,1:T(8,128)(2,1)}), bf16[1,16,128,512]{3,2,0,1:T(8,128)(2,1)S(1)}, u32[]{:S(2)}, u32[]{:S(2)}) async-start(bf16[1,16,128,512]{3,2,0,1:T(8,128)(2,1)} %bitcast.200), calls=%async_computation.6 | async-start | bytes 4194304 | tf_op jit(solution)/shard_map/all_to_all | solution.py:27
  283.3 1.3 copy-start.5
  284.6 52.1 %all-to-all-start.3 = ((bf16[1,2,1024,512]{3,1,0,2:T(2,128)(2,1)}), bf16[1,2,1024,512]{3,1,0,2:T(2,128)(2,1)S(1)}, u32[]{:S(2)}, u32[]{:S(2)}) async-start(bf16[1,2,1024,512]{3,1,0,2:T(2,128)(2,1)} %copy.100), calls=%async_computation.3 | async-start | bytes 4194304 | tf_op jit(solution)/shard_map/all_to_all | solution.py:27
  336.7 1.3 copy-start.4
  338.0 52.5 %all-to-all-start.7 = ((bf16[1,2,1024,512]{3,1,0,2:T(2,128)(2,1)}), bf16[1,2,1024,512]{3,1,0,2:T(2,128)(2,1)}, u32[]{:S(2)}, u32[]{:S(2)}) async-start(bf16[1,2,1024,512]{3,1,0,2:T(2,128)(2,1)} %copy.109), calls=%async_computation.7 | async-start | bytes 4194304 | tf_op jit(solution)/shard_map/all_to_all | solution.py:27
  344.4 18.9 %copy-start.11 = (f32[2,3,3,3]{3,0,2,1:T(2,128)S(1)}, f32[2,3,3,3]{3,0,2,1:T(2,128)}, u32[]{:S(2)}) copy-start(f32[2,3,3,3]{3,0,2,1:T(2,128)} %param.11) | copy-start | bytes 652
  344.5 15.9 %collective-permute-start = (bf16[16,1,512]{2,1,0:T(2,128)(2,1)S(1)}, bf16[16,1,512]{2,1,0:T(2,128)(2,1)S(1)}, u32[]{:S(2)}, u32[]{:S(2)}) collective-permute-start(bf16[16,1,512]{2,1,0:T(2,128)(2,1)S(1)} %get-tuple-element.16), channel_id=1, source_target_pairs={{0,4},{4,8},{8,12},{12,16},{16,20},{20,24},{24,28},{1,5},{5,9},{9,... | collective-permute-start | bytes 49160 | tf_op jit(solution)/shard_map/ppermute | solution.py:20
  348.3 12.2 %collective-permute-start.1 = (bf16[16,1,512]{2,1,0:T(2,128)(2,1)S(1)}, bf16[16,1,512]{2,1,0:T(2,128)(2,1)S(1)}, u32[]{:S(2)}, u32[]{:S(2)}) collective-permute-start(bf16[16,1,512]{2,1,0:T(2,128)(2,1)S(1)} %get-tuple-element.17), channel_id=1, source_target_pairs={{4,0},{8,4},{12,8},{16,12},{20,16},{24,20},{28,24},{5,1},{9,5},{13... | collective-permute-start | bytes 49160 | tf_op jit(solution)/shard_map/ppermute | solution.py:21
  360.5 32.3 %collective-permute-start.2 = (bf16[1,130,512]{2,1,0:T(8,128)(2,1)S(1)}, bf16[1,130,512]{2,1,0:T(8,128)(2,1)S(1)}, u32[]{:S(2)}, u32[]{:S(2)}) collective-permute-start(bf16[1,130,512]{2,1,0:T(8,128)(2,1)S(1)} %get-tuple-element.14), channel_id=1, source_target_pairs={{0,1},{1,2},{2,3},{4,5},{5,6},{6,7},{8,9},{9,10},{10,11},{12,13},{... | collective-permute-start | bytes 399368 | tf_op jit(solution)/shard_map/ppermute | solution.py:20
  361.8 31.0 %collective-permute-start.3 = (bf16[1,130,512]{2,1,0:T(8,128)(2,1)S(1)}, bf16[1,130,512]{2,1,0:T(8,128)(2,1)S(1)}, u32[]{:S(2)}, u32[]{:S(2)}) collective-permute-start(bf16[1,130,512]{2,1,0:T(8,128)(2,1)S(1)} %get-tuple-element.15), channel_id=1, source_target_pairs={{1,0},{2,1},{3,2},{5,4},{6,5},{7,6},{9,8},{10,9},{11,10},{13,12},{... | collective-permute-start | bytes 399368 | tf_op jit(solution)/shard_map/ppermute | solution.py:21
  392.8 46.3 %copy-start.1 = (f32[1,2,8,128,512]{4,3,1,2,0:T(8,128)}, f32[1,2,8,128,512]{4,3,1,2,0:T(8,128)S(1)}, u32[]{:S(2)}) copy-start(f32[1,2,8,128,512]{4,3,1,2,0:T(8,128)S(1)} %copy.110) | copy-start | bytes 12582916
  439.0 1.6 collective-permute-start.10
  439.1 16.0 %copy-start.9 = (f32[2,128,512]{2,1,0:T(8,128)S(1)}, f32[2,128,512]{2,1,0:T(8,128)}, u32[]{:S(2)}) copy-start(f32[2,128,512]{2,1,0:T(8,128)} %param.7) | copy-start | bytes 1572868
  440.2 15.0 %copy-start.2 = (f32[1,2,8,128,512]{4,3,1,2,0:T(8,128)S(1)}, f32[1,2,8,128,512]{4,3,1,2,0:T(8,128)}, u32[]{:S(2)}) copy-start(f32[1,2,8,128,512]{4,3,1,2,0:T(8,128)} %copy-done.1) | copy-start | bytes 12582916
  440.7 1.6 collective-permute-start.4
  440.9 9.1 %collective-permute-start.11 = (f32[128,512]{1,0:T(8,128)S(1)}, f32[128,512]{1,0:T(8,128)S(1)}, u32[]{:S(2)}, u32[]{:S(2)}) collective-permute-start(f32[128,512]{1,0:T(8,128)S(1)} %get-tuple-element.20), channel_id=1, source_target_pairs={{0,2},{1,3},{2,0},{3,1},{4,6},{5,7},{6,4},{7,5},{8,10},{9,11},{10,... | collective-permute-start | bytes 786440 | tf_op jit(solution)/shard_map/ppermute | solution.py:36
  442.3 12.8 %collective-permute-start.5 = (f32[128,512]{1,0:T(8,128)S(1)}, f32[128,512]{1,0:T(8,128)S(1)}, u32[]{:S(2)}, u32[]{:S(2)}) collective-permute-start(f32[128,512]{1,0:T(8,128)S(1)} %add.78), channel_id=1, source_target_pairs={{0,2},{1,3},{2,0},{3,1},{4,6},{5,7},{6,4},{7,5},{8,10},{9,11},{10,... | collective-permute-start | bytes 786440 | tf_op jit(solution)/shard_map/ppermute | solution.py:36
  458.5 78.1 %all-to-all-start.12 = ((bf16[1,16,128,512]{3,2,0,1:T(8,128)(2,1)}), bf16[1,16,128,512]{3,2,0,1:T(8,128)(2,1)}, u32[]{:S(2)}, u32[]{:S(2)}) async-start(bf16[1,16,128,512]{3,2,0,1:T(8,128)(2,1)} %get-tuple-element.23), calls=%async_computation.12 | async-start | bytes 4194304 | tf_op jit(solution)/shard_map/all_to_all | solution.py:27
  467.9 18.0 %collective-permute-start.6 = (bf16[2,16,1,512]{3,2,1,0:T(2,128)(2,1)S(1)}, bf16[2,16,1,512]{3,2,1,0:T(2,128)(2,1)S(1)}, u32[]{:S(2)}, u32[]{:S(2)}) collective-permute-start(bf16[2,16,1,512]{3,2,1,0:T(2,128)(2,1)S(1)} %get-tuple-element.10), channel_id=1, source_target_pairs={{0,4},{4,8},{8,12},{12,16},{16,20},{20,24},{24,28},{1,5},{5,9},{9,... | collective-permute-start | bytes 98312 | tf_op jit(solution)/shard_map/ppermute | solution.py:20
  471.8 14.0 %collective-permute-start.7 = (bf16[2,16,1,512]{3,2,1,0:T(2,128)(2,1)S(1)}, bf16[2,16,1,512]{3,2,1,0:T(2,128)(2,1)S(1)}, u32[]{:S(2)}, u32[]{:S(2)}) collective-permute-start(bf16[2,16,1,512]{3,2,1,0:T(2,128)(2,1)S(1)} %get-tuple-element.11), channel_id=1, source_target_pairs={{4,0},{8,4},{12,8},{16,12},{20,16},{24,20},{28,24},{5,1},{9,5},{13... | collective-permute-start | bytes 98312 | tf_op jit(solution)/shard_map/ppermute | solution.py:21
  486.0 2.6 collective-permute-start.8
  487.3 4.3 collective-permute-start.9
  536.6 81.3 %all-to-all-start.8 = ((bf16[1,16,128,512]{3,2,0,1:T(8,128)(2,1)}), bf16[1,16,128,512]{3,2,0,1:T(8,128)(2,1)S(1)}, u32[]{:S(2)}, u32[]{:S(2)}) async-start(bf16[1,16,128,512]{3,2,0,1:T(8,128)(2,1)} %bitcast.42), calls=%async_computation.8 | async-start | bytes 4194304 | tf_op jit(solution)/shard_map/all_to_all | solution.py:27
  617.9 1.3 copy-start.6
  619.3 55.2 %all-to-all-start.13 = ((bf16[1,2,1024,512]{3,1,0,2:T(2,128)(2,1)}), bf16[1,2,1024,512]{3,1,0,2:T(2,128)(2,1)S(1)}, u32[]{:S(2)}, u32[]{:S(2)}) async-start(bf16[1,2,1024,512]{3,1,0,2:T(2,128)(2,1)} %copy.124), calls=%async_computation.13 | async-start | bytes 4194304 | tf_op jit(solution)/shard_map/all_to_all | solution.py:27
  674.5 52.6 %all-to-all-start.9 = ((bf16[1,2,1024,512]{3,1,0,2:T(2,128)(2,1)}), bf16[1,2,1024,512]{3,1,0,2:T(2,128)(2,1)}, u32[]{:S(2)}, u32[]{:S(2)}) async-start(bf16[1,2,1024,512]{3,1,0,2:T(2,128)(2,1)} %copy.113), calls=%async_computation.9 | async-start | bytes 4194304 | tf_op jit(solution)/shard_map/all_to_all | solution.py:27
  727.1 29.3 %all-to-all-start.14 = ((bf16[1,16,128,512]{3,1,0,2:T(8,128)(2,1)}), bf16[1,16,128,512]{3,1,0,2:T(8,128)(2,1)S(1)}, u32[]{:S(2)}, u32[]{:S(2)}) async-start(bf16[1,16,128,512]{3,1,0,2:T(8,128)(2,1)} %copy.127), calls=%async_computation.14 | async-start | bytes 4194304 | tf_op jit(solution)/shard_map/all_to_all | solution.py:27
  756.4 1.3 copy-start.8
  757.7 29.5 %all-to-all-start.10 = ((bf16[1,16,128,512]{3,1,0,2:T(8,128)(2,1)}), bf16[1,16,128,512]{3,1,0,2:T(8,128)(2,1)S(1)}, u32[]{:S(2)}, u32[]{:S(2)}) async-start(bf16[1,16,128,512]{3,1,0,2:T(8,128)(2,1)} %copy.116), calls=%async_computation.10 | async-start | bytes 4194304 | tf_op jit(solution)/shard_map/all_to_all | solution.py:27
  787.2 1.3 copy-start.7
  788.5 29.3 %all-to-all-start.15 = ((bf16[1,64,32,512]{3,2,0,1:T(8,128)(2,1)}), bf16[1,64,32,512]{3,2,0,1:T(8,128)(2,1)S(1)}, u32[]{:S(2)}, u32[]{:S(2)}) async-start(bf16[1,64,32,512]{3,2,0,1:T(8,128)(2,1)} %copy.131), calls=%async_computation.15 | async-start | bytes 4194304 | tf_op jit(solution)/shard_map/all_to_all | solution.py:27
  817.8 30.5 %all-to-all-start.11 = ((bf16[1,64,32,512]{3,2,0,1:T(8,128)(2,1)}), bf16[1,64,32,512]{3,2,0,1:T(8,128)(2,1)}, u32[]{:S(2)}, u32[]{:S(2)}) async-start(bf16[1,64,32,512]{3,2,0,1:T(8,128)(2,1)} %copy.120), calls=%async_computation.11 | async-start | bytes 4194304 | tf_op jit(solution)/shard_map/all_to_all | solution.py:27
  850.2 3.8 copy-start.3
Sparse Core Ops, SparseCore 0:
  164.9 70.8 all-gather.1

commit v3 on v2

--- a/solution.py
+++ b/solution.py
@@ -24,7 +24,25 @@
 
 
 def moved(values, axis, split, concat):
-    return lax.all_to_all(values, axis, split_axis=split, concat_axis=concat, tiled=True)
+    peers, me = lax.axis_size(axis), lax.axis_index(axis)
+    if axis == "gx" or peers > 8:
+        return lax.all_to_all(values, axis, split_axis=split, concat_axis=concat, tiled=True)
+    width, length = values.shape[split] // peers, values.shape[concat]
+
+    def piece(owner):
+        return lax.dynamic_slice_in_dim(values, owner * width, width, axis=split)
+
+    shape = list(values.shape)
+    shape[split], shape[concat] = width, length * peers
+    parts = [(me, piece(me))]
+    for step in range(1, peers):
+        ring = [(i, (i + step) % peers) for i in range(peers)]
+        sent = lax.ppermute(piece(lax.rem(me + step, peers)), axis, ring)
+        parts.append((lax.rem(me + peers - step, peers), sent))
+    whole = jnp.zeros(shape, values.dtype)
+    for owner, part in parts:
+        whole = lax.dynamic_update_slice_in_dim(whole, part, owner * length, axis=concat)
+    return whole
 
 
 def total(values, axis):

time: 876 us -> 765 us (0.87)
  waiting for transfers between devices: 407 us -> 325 us
  blocking collectives: 62.1 us -> 31.7 us
    all_to_all x15 -> x8, waiting for transfers between devices: 366 us -> 160 us  [moved(): lax.all_to_all(values, axis, split_axis=split, concat_axis=concat, tiled=...]
    ppermute x0 -> x24, waiting for transfers between devices: none -> 94.5 us  [moved(): sent = lax.ppermute(piece(lax.rem(me + step, peers)), axis, ring)]
    all_gather x1, waiting for transfers between devices: 0.01 us -> 31.9 us  [local(): lax.all_gather(lower_x, 'gx', axis=0, tiled=True)]
    all_to_all x1 -> x0, blocking collectives: 29.8 us -> none  [moved(): lax.all_to_all(values, axis, split_axis=split, concat_axis=concat, tiled=...]
    dynamic_update_slice x0 -> x32, local copies, waits for them, and re-layouts: none -> 27 us  [moved(): lax.dynamic_update_slice_in_dim(whole, part, owner * length, axis=concat)]
    all_to_all x15 -> x8, starting transfers between devices: 98.9 us -> 74.8 us  [moved(): lax.all_to_all(values, axis, split_axis=split, concat_axis=concat, tiled=...]
    ppermute x0 -> x24, starting transfers between devices: none -> 21.5 us  [moved(): sent = lax.ppermute(piece(lax.rem(me + step, peers)), axis, ring)]
    all_to_all x23 -> x9, local copies, waits for them, and re-layouts: 47.3 us -> 32 us  [moved(): lax.all_to_all(values, axis, split_axis=split, concat_axis=concat, tiled=...]
  transfers between devices with their start and end apart: 28 -> 45, of which waited for: 20 -> 31; matrix products, arithmetic and copies ran while one was open for 17% -> 19% of each run, Pallas kernels for 5% -> 6%
where the time goes in v3:
time: 765 us; the launch traced here: 751 us
  waiting for transfers between devices  325 us (42%)
  local copies, waits for them, and re-layouts  122 us (16%)
  starting transfers between devices  115 us (15%)
  Pallas kernels  88.4 us (12%)
  matrix products  36.6 us (5%)
  blocking collectives  31.7 us (4%)
  other arithmetic  17.6 us (2%)
  between operations  15.1 us (2%)
    all_to_all x8, waiting for transfers between devices, moved(): lax.all_to_all(values, axis, split_axis=split, concat_axis=concat, tiled=...  160 us
    ppermute x24, waiting for transfers between devices, moved(): sent = lax.ppermute(piece(lax.rem(me + step, peers)), axis, ring)  94.5 us
    all_to_all x8, starting transfers between devices, moved(): lax.all_to_all(values, axis, split_axis=split, concat_axis=concat, tiled=...  74.8 us
    pallas_call x1, Pallas kernels, coupling_forward(): pl.pallas_call(forward_kernel, grid=(depth,), in_specs=[smem, smem, *plan...  45.2 us
    pallas_call x1, Pallas kernels, coupling_backward(): pl.pallas_call(backward_kernel, grid=(depth,), in_specs=[smem, smem, *pla...  43.2 us
    all_to_all x9, local copies, waits for them, and re-layouts, moved(): lax.all_to_all(values, axis, split_axis=split, concat_axis=concat, tiled=...  32 us
    all_gather x1, waiting for transfers between devices, local(): lax.all_gather(lower_x, 'gx', axis=0, tiled=True)  31.9 us
    all_gather x1, blocking collectives, local(): lax.all_gather(lower_y, 'gx', axis=0, tiled=True)  31.7 us
  transfers between devices with their start and end apart: 45, of which 31 were waited for; matrix products, arithmetic and copies ran while one was open for 19% of the time, Pallas kernels for 6%

profile of v3, /device:TPU:0, one launch (start us, length us, event | category | flops | bytes accessed | tf_op | source)
XLA Modules:
  0.0 751.5 jit_solution(2624855079611591937)
XLA Ops:
  7.2 4.0 convert_element_type.115
  19.0 31.7 %all_gather.6 = bf16[512,512]{1,0:T(8,128)(2,1)S(1)} all-gather(bf16[64,512]{1,0:T(8,128)(2,1)S(1)} %copy-done.6), channel_id=1, replica_groups=mesh['gx'=8,'gz'=4] {'gx'}, dimensions={0}, use_global_device_ids=true | all-gather | bytes 589824 | tf_op jit(solution)/shard_map/all_gather | solution.py:194
  53.7 3.1 fusion.46
  63.3 9.0 %collective-permute-done.3 = bf16[1,16,32,512]{3,1,2,0:T(8,128)(2,1)S(1)} collective-permute-done((bf16[1,16,32,512]{3,1,2,0:T(8,128)(2,1)S(1)}, bf16[1,16,32,512]{3,1,2,0:T(8,128)(2,1)S(1)}, u32[]{:S(2)}, u32[]{:S(2)}) %collective-permute-start.3) | collective-permute-done | bytes 524320 | tf_op jit(solution)/shard_map/ppermute | solution.py:40
  74.5 7.6 %collective-permute-done.5 = bf16[1,16,32,512]{3,1,2,0:T(8,128)(2,1)S(1)} collective-permute-done((bf16[1,16,32,512]{3,1,2,0:T(8,128)(2,1)S(1)}, bf16[1,16,32,512]{3,1,2,0:T(8,128)(2,1)S(1)}, u32[]{:S(2)}, u32[]{:S(2)}) %collective-permute-start.5) | collective-permute-done | bytes 524320 | tf_op jit(solution)/shard_map/ppermute | solution.py:40
  83.2 5.5 all-to-all-start
  96.7 6.2 collective-permute-done.10
  104.0 3.4 collective-permute-done.11
  108.5 6.9 collective-permute-done.12
  116.5 4.7 fusion.49
  121.2 2.7 dynamic-slice_bitcast_fusion.8
  129.8 7.8 %collective-permute-done.13 = bf16[1,16,32,512]{3,1,2,0:T(8,128)(2,1)} collective-permute-done((bf16[1,16,32,512]{3,1,2,0:T(8,128)(2,1)}, bf16[1,16,32,512]{3,1,2,0:T(8,128)(2,1)}, u32[]{:S(2)}, u32[]{:S(2)}) %collective-permute-start.13) | collective-permute-done | bytes 524320 | tf_op jit(solution)/shard_map/ppermute | solution.py:40
  142.4 5.8 collective-permute-done.15
  149.4 5.7 all-to-all-start.2
  155.0 2.6 copy.94
  157.6 2.8 reshape.257
  160.4 31.9 %all-gather.2.cloned.1.call-done = bf16[1024,1024]{1,0:T(8,128)(2,1)} async-done(((bf16[128,1024]{1,0:T(8,128)(2,1)}), bf16[1024,1024]{1,0:T(8,128)(2,1)}) %all-gather.2.cloned.1.call-update) | async-done | bytes 2097168 | tf_op jit(solution)/shard_map/all_gather | solution.py:193
  192.4 5.3 convert_bitcast_fusion.3
  197.6 6.2 copy.95
  203.8 15.0 %all-to-all-done.2 = bf16[1,16,128,512]{3,2,0,1:T(8,128)(2,1)} async-done(((bf16[1,16,128,512]{3,2,0,1:T(8,128)(2,1)}), bf16[1,16,128,512]{3,2,0,1:T(8,128)(2,1)}, u32[]{:S(2)}, u32[]{:S(2)}) %all-to-all-start.2) | async-done | bytes 2097184 | tf_op jit(solution)/shard_map/all_to_all | solution.py:29
  218.8 3.7 all-to-all-start.1
  222.6 4.3 copy.105
  226.9 4.2 reshape.266
  231.1 5.9 convert_bitcast_fusion.2
  237.0 6.2 copy.106
  243.2 28.0 %all-to-all-done.1 = bf16[1,2,1024,512]{3,1,0,2:T(2,128)(2,1)S(1)} async-done(((bf16[1,2,1024,512]{3,1,0,2:T(2,128)(2,1)}), bf16[1,2,1024,512]{3,1,0,2:T(2,128)(2,1)S(1)}, u32[]{:S(2)}, u32[]{:S(2)}) %all-to-all-start.1) | async-done | bytes 2097184 | tf_op jit(solution)/shard_map/all_to_all | solution.py:29
  272.5 4.4 all-to-all-start.3
  279.0 3.8 collective-permute-start.6
  284.1 10.9 %collective-permute-done.6 = bf16[16,1,512]{2,1,0:T(2,128)(2,1)S(1)} collective-permute-done((bf16[16,1,512]{2,1,0:T(2,128)(2,1)S(1)}, bf16[16,1,512]{2,1,0:T(2,128)(2,1)S(1)}, u32[]{:S(2)}, u32[]{:S(2)}) %collective-permute-start.6) | collective-permute-done | bytes 16416 | tf_op jit(solution)/shard_map/ppermute | solution.py:20
  298.0 27.0 %all-to-all-done.3 = bf16[1,2,1024,512]{3,1,0,2:T(2,128)(2,1)} async-done(((bf16[1,2,1024,512]{3,1,0,2:T(2,128)(2,1)}), bf16[1,2,1024,512]{3,1,0,2:T(2,128)(2,1)}, u32[]{:S(2)}, u32[]{:S(2)}) %all-to-all-start.3) | async-done | bytes 2097184 | tf_op jit(solution)/shard_map/all_to_all | solution.py:29
  328.2 45.2 %shard_map.77 = (f32[16,128,512]{2,1,0:T(8,128)S(1)}, f32[16,128,512]{2,1,0:T(8,128)S(1)}, f32[2,128,512]{2,1,0:T(8,128)S(1)}) custom-call(f32[54]{0:T(128)S(1)} %reshape.248.taps, f32[2,16]{1,0:T(2,128)S(1)} %pad_maximum_fusion.11.weights, f32[18,144,512]{2,1,0:T(8,128)S(1)} %fusion.15.p0.p1.p2, f32[18,144,512]{2,1,0:T(8,128)S(1)} %fusion.15.p0.p1.p2, ...), custom_call_target="tpu_custom_call" | custom-call | flops 1258291200 | bytes 25165824 | tf_op jit(solution)/shard_map/pallas_call | solution.py:153
  378.6 5.8 collective-permute-done.23
  384.5 5.1 collective-permute-done.17
  389.8 3.3 fusion.11
  393.0 10.6 %all-to-all-start.6 = ((bf16[1,16,128,512]{3,2,0,1:T(8,128)(2,1)}), bf16[1,16,128,512]{3,2,0,1:T(8,128)(2,1)}, u32[]{:S(2)}, u32[]{:S(2)}) async-start(bf16[1,16,128,512]{3,2,0,1:T(8,128)(2,1)} %get-tuple-element.53), calls=%async_computation.6 | async-start | bytes 4194304 | tf_op jit(solution)/shard_map/all_to_all | solution.py:29
  404.3 3.9 collective-permute-start.18
  409.5 12.7 %collective-permute-done.18 = bf16[2,16,1,512]{3,2,1,0:T(2,128)(2,1)S(1)} collective-permute-done((bf16[2,16,1,512]{3,2,1,0:T(2,128)(2,1)S(1)}, bf16[2,16,1,512]{3,2,1,0:T(2,128)(2,1)S(1)}, u32[]{:S(2)}, u32[]{:S(2)}) %collective-permute-start.18) | collective-permute-done | bytes 32800 | tf_op jit(solution)/shard_map/ppermute | solution.py:20
  425.0 3.0 collective-permute-done.21
  429.8 43.2 %shard_map.78 = bf16[16,128,512]{2,1,0:T(8,128)(2,1)} custom-call(f32[54]{0:T(128)S(1)} %reshape.248.taps, f32[2,16]{1,0:T(2,128)S(1)} %pad_maximum_fusion.11.weights, f32[2,18,144,512]{3,2,1,0:T(8,128)S(1)} %fusion.1.p0.p1.p2, f32[2,18,144,512]{3,2,1,0:T(8,128)S(1)} %fusion.1.p0.p1.p2, f32[2,18,144,512]{3,2,1,0:T(8,128)S(1)} %fusion.1.p0.p1.p2, ...), custom_call_target="tpu_custom_call" | custom-call | flops 1258291200 | bytes 33554432 | tf_op jit(solution)/shard_map/pallas_call | solution.py:169
  473.0 34.4 %all-to-all-start.4 = ((bf16[1,16,128,512]{3,2,0,1:T(8,128)(2,1)}), bf16[1,16,128,512]{3,2,0,1:T(8,128)(2,1)S(1)}, u32[]{:S(2)}, u32[]{:S(2)}) async-start(bf16[1,16,128,512]{3,2,0,1:T(8,128)(2,1)} %bitcast.48), calls=%async_computation.4 | async-start | bytes 4194304 | tf_op jit(solution)/shard_map/all_to_all | solution.py:29
  507.4 4.3 copy.118
  511.7 4.2 reshape.280
  515.9 5.9 convert_bitcast_fusion
  521.7 6.2 copy.119
  527.9 26.4 %all-to-all-done.4 = bf16[1,16,128,512]{3,2,0,1:T(8,128)(2,1)S(1)} async-done(((bf16[1,16,128,512]{3,2,0,1:T(8,128)(2,1)}), bf16[1,16,128,512]{3,2,0,1:T(8,128)(2,1)S(1)}, u32[]{:S(2)}, u32[]{:S(2)}) %all-to-all-start.4) | async-done | bytes 2097184 | tf_op jit(solution)/shard_map/all_to_all | solution.py:29
  555.6 6.2 all-to-all-start.7
  561.8 4.4 copy.109
  566.1 4.2 reshape.267
  570.3 5.9 convert_bitcast_fusion.1
  576.2 6.2 copy.110
  582.3 28.5 %all-to-all-done.7 = bf16[1,2,1024,512]{3,1,0,2:T(2,128)(2,1)S(1)} async-done(((bf16[1,2,1024,512]{3,1,0,2:T(2,128)(2,1)}), bf16[1,2,1024,512]{3,1,0,2:T(2,128)(2,1)S(1)}, u32[]{:S(2)}, u32[]{:S(2)}) %all-to-all-start.7) | async-done | bytes 2097184 | tf_op jit(solution)/shard_map/all_to_all | solution.py:29
  610.8 4.4 all-to-all-start.5
  615.2 3.7 copy.120
  618.9 2.7 all_to_all.111
  627.9 35.5 %all-to-all-done.5 = bf16[1,2,1024,512]{3,1,0,2:T(2,128)(2,1)} async-done(((bf16[1,2,1024,512]{3,1,0,2:T(2,128)(2,1)}), bf16[1,2,1024,512]{3,1,0,2:T(2,128)(2,1)}, u32[]{:S(2)}, u32[]{:S(2)}) %all-to-all-start.5) | async-done | bytes 2097184 | tf_op jit(solution)/shard_map/all_to_all | solution.py:29
  663.4 5.3 copy.111
  668.7 2.7 all_to_all.104
  686.8 8.8 %collective-permute-done.26 = bf16[1,16,32,512]{3,1,2,0:T(8,128)(2,1)S(1)} collective-permute-done((bf16[1,16,32,512]{3,1,2,0:T(8,128)(2,1)S(1)}, bf16[1,16,32,512]{3,1,2,0:T(8,128)(2,1)S(1)}, u32[]{:S(2)}, u32[]{:S(2)}) %collective-permute-start.26) | collective-permute-done | bytes 524320 | tf_op jit(solution)/shard_map/ppermute | solution.py:40
  696.6 2.6 collective-permute-start.27
  699.8 7.6 %collective-permute-done.33 = bf16[1,16,32,512]{3,1,2,0:T(8,128)(2,1)S(1)} collective-permute-done((bf16[1,16,32,512]{3,1,2,0:T(8,128)(2,1)S(1)}, bf16[1,16,32,512]{3,1,2,0:T(8,128)(2,1)S(1)}, u32[]{:S(2)}, u32[]{:S(2)}) %collective-permute-start.33) | collective-permute-done | bytes 524320 | tf_op jit(solution)/shard_map/ppermute | solution.py:40
  709.6 8.5 %collective-permute-done.35 = bf16[1,16,32,512]{3,1,2,0:T(8,128)(2,1)S(1)} collective-permute-done((bf16[1,16,32,512]{3,1,2,0:T(8,128)(2,1)S(1)}, bf16[1,16,32,512]{3,1,2,0:T(8,128)(2,1)S(1)}, u32[]{:S(2)}, u32[]{:S(2)}) %collective-permute-start.35) | collective-permute-done | bytes 524320 | tf_op jit(solution)/shard_map/ppermute | solution.py:40
  719.8 10.1 %collective-permute-done.27 = bf16[1,16,32,512]{3,1,2,0:T(8,128)(2,1)S(1)} collective-permute-done((bf16[1,16,32,512]{3,1,2,0:T(8,128)(2,1)S(1)}, bf16[1,16,32,512]{3,1,2,0:T(8,128)(2,1)S(1)}, u32[]{:S(2)}, u32[]{:S(2)}) %collective-permute-start.27) | collective-permute-done | bytes 524320 | tf_op jit(solution)/shard_map/ppermute | solution.py:40
  732.0 6.1 collective-permute-done.29
  739.8 4.4 pad_maximum_fusion
  (149 shorter events, 98.3 us)
Async XLA Ops:
  7.2 46.5 %copy-start = (bf16[64,64]{1,0:T(8,128)(2,1)S(1)}, bf16[64,64]{1,0:T(8,128)(2,1)}, u32[]{:S(2)}) copy-start(bf16[64,64]{1,0:T(8,128)(2,1)} %param.10) | copy-start | bytes 24580
  14.0 5.0 copy-start.6
  14.0 36.6 %collective-permute-start = (bf16[1,16,32,512]{3,2,1,0:T(8,128)(2,1)}, bf16[1,16,32,512]{3,2,1,0:T(8,128)(2,1)}, u32[]{:S(2)}, u32[]{:S(2)}) collective-permute-start(bf16[1,16,32,512]{3,2,1,0:T(8,128)(2,1)} %get-tuple-element.46), channel_id=1, source_target_pairs={{0,1},{1,2},{2,3},{3,0},{4,5},{5,6},{6,7},{7,4},{8,9},{9,10},{10,1... | collective-permute-start | bytes 1572872 | tf_op jit(solution)/shard_map/ppermute | solution.py:40
  14.4 37.6 %collective-permute-start.1 = (bf16[1,16,32,512]{3,2,1,0:T(8,128)(2,1)}, bf16[1,16,32,512]{3,2,1,0:T(8,128)(2,1)}, u32[]{:S(2)}, u32[]{:S(2)}) collective-permute-start(bf16[1,16,32,512]{3,2,1,0:T(8,128)(2,1)} %get-tuple-element.45), channel_id=1, source_target_pairs={{0,2},{1,3},{2,0},{3,1},{4,6},{5,7},{6,4},{7,5},{8,10},{9,11},{10,... | collective-permute-start | bytes 1572872 | tf_op jit(solution)/shard_map/ppermute | solution.py:40
  16.9 36.4 %collective-permute-start.2 = (bf16[1,16,32,512]{3,2,1,0:T(8,128)(2,1)}, bf16[1,16,32,512]{3,2,1,0:T(8,128)(2,1)S(1)}, u32[]{:S(2)}, u32[]{:S(2)}) collective-permute-start(bf16[1,16,32,512]{3,2,1,0:T(8,128)(2,1)} %get-tuple-element.44), channel_id=1, source_target_pairs={{0,3},{1,0},{2,1},{3,2},{4,7},{5,4},{6,5},{7,6},{8,11},{9,8},{10,9... | collective-permute-start | bytes 1572872 | tf_op jit(solution)/shard_map/ppermute | solution.py:40
  58.6 13.7 %collective-permute-start.3 = (bf16[1,16,32,512]{3,1,2,0:T(8,128)(2,1)S(1)}, bf16[1,16,32,512]{3,1,2,0:T(8,128)(2,1)S(1)}, u32[]{:S(2)}, u32[]{:S(2)}) collective-permute-start(bf16[1,16,32,512]{3,1,2,0:T(8,128)(2,1)S(1)} %get-tuple-element.42), channel_id=1, source_target_pairs={{0,1},{1,2},{2,3},{3,0},{4,5},{5,6},{6,7},{7,4},{8,9},{9,10},{10,1... | collective-permute-start | bytes 1572872 | tf_op jit(solution)/shard_map/ppermute | solution.py:40
  58.6 14.8 %collective-permute-start.4 = (bf16[1,16,32,512]{3,1,2,0:T(8,128)(2,1)S(1)}, bf16[1,16,32,512]{3,1,2,0:T(8,128)(2,1)S(1)}, u32[]{:S(2)}, u32[]{:S(2)}) collective-permute-start(bf16[1,16,32,512]{3,1,2,0:T(8,128)(2,1)S(1)} %get-tuple-element.41), channel_id=1, source_target_pairs={{0,2},{1,3},{2,0},{3,1},{4,6},{5,7},{6,4},{7,5},{8,10},{9,11},{10,... | collective-permute-start | bytes 1572872 | tf_op jit(solution)/shard_map/ppermute | solution.py:40
  59.3 22.9 %collective-permute-start.5 = (bf16[1,16,32,512]{3,1,2,0:T(8,128)(2,1)S(1)}, bf16[1,16,32,512]{3,1,2,0:T(8,128)(2,1)S(1)}, u32[]{:S(2)}, u32[]{:S(2)}) collective-permute-start(bf16[1,16,32,512]{3,1,2,0:T(8,128)(2,1)S(1)} %get-tuple-element.40), channel_id=1, source_target_pairs={{0,3},{1,0},{2,1},{3,2},{4,7},{5,4},{6,5},{7,6},{8,11},{9,8},{10,9... | collective-permute-start | bytes 1572872 | tf_op jit(solution)/shard_map/ppermute | solution.py:40
  83.2 66.1 %all-to-all-start = ((bf16[1,16,128,512]{3,2,0,1:T(8,128)(2,1)}), bf16[1,16,128,512]{3,2,0,1:T(8,128)(2,1)S(1)}, u32[]{:S(2)}, u32[]{:S(2)}) async-start(bf16[1,16,128,512]{3,2,0,1:T(8,128)(2,1)} %copy_dynamic-update-slice_fusion.16), calls=%async_computation | async-start | bytes 4194304 | tf_op jit(solution)/shard_map/all_to_all | solution.py:29
  88.8 103.6 %all-gather.2.cloned.1.call-start = ((), (), s32[]{:S(2)}) async-start(), calls=%async_computation.8 | async-start | bytes 2359296 | tf_op jit(solution)/shard_map/all_gather | solution.py:193
  90.5 12.4 %collective-permute-start.10 = (bf16[1,16,32,512]{3,2,1,0:T(8,128)(2,1)S(1)}, bf16[1,16,32,512]{3,2,1,0:T(8,128)(2,1)S(1)}, u32[]{:S(2)}, u32[]{:S(2)}) collective-permute-start(bf16[1,16,32,512]{3,2,1,0:T(8,128)(2,1)S(1)} %get-tuple-element.36), channel_id=1, source_target_pairs={{0,1},{1,2},{2,3},{3,0},{4,5},{5,6},{6,7},{7,4},{8,9},{9,10},{10,1... | collective-permute-start | bytes 1572872 | tf_op jit(solution)/shard_map/ppermute | solution.py:40
  92.5 14.9 %collective-permute-start.11 = (bf16[1,16,32,512]{3,2,1,0:T(8,128)(2,1)S(1)}, bf16[1,16,32,512]{3,2,1,0:T(8,128)(2,1)S(1)}, u32[]{:S(2)}, u32[]{:S(2)}) collective-permute-start(bf16[1,16,32,512]{3,2,1,0:T(8,128)(2,1)S(1)} %get-tuple-element.35), channel_id=1, source_target_pairs={{0,2},{1,3},{2,0},{3,1},{4,6},{5,7},{6,4},{7,5},{8,10},{9,11},{10,... | collective-permute-start | bytes 1572872 | tf_op jit(solution)/shard_map/ppermute | solution.py:40
  93.1 22.3 %collective-permute-start.12 = (bf16[1,16,32,512]{3,2,1,0:T(8,128)(2,1)S(1)}, bf16[1,16,32,512]{3,2,1,0:T(8,128)(2,1)S(1)}, u32[]{:S(2)}, u32[]{:S(2)}) collective-permute-start(bf16[1,16,32,512]{3,2,1,0:T(8,128)(2,1)S(1)} %get-tuple-element.34), channel_id=1, source_target_pairs={{0,3},{1,0},{2,1},{3,2},{4,7},{5,4},{6,5},{7,6},{8,11},{9,8},{10,9... | collective-permute-start | bytes 1572872 | tf_op jit(solution)/shard_map/ppermute | solution.py:40
  123.9 13.7 %collective-permute-start.13 = (bf16[1,16,32,512]{3,1,2,0:T(8,128)(2,1)}, bf16[1,16,32,512]{3,1,2,0:T(8,128)(2,1)}, u32[]{:S(2)}, u32[]{:S(2)}) collective-permute-start(bf16[1,16,32,512]{3,1,2,0:T(8,128)(2,1)} %get-tuple-element.32), channel_id=1, source_target_pairs={{0,1},{1,2},{2,3},{3,0},{4,5},{5,6},{6,7},{7,4},{8,9},{9,10},{10,1... | collective-permute-start | bytes 1572872 | tf_op jit(solution)/shard_map/ppermute | solution.py:40
  125.1 15.1 %collective-permute-start.14 = (bf16[1,16,32,512]{3,1,2,0:T(8,128)(2,1)}, bf16[1,16,32,512]{3,1,2,0:T(8,128)(2,1)}, u32[]{:S(2)}, u32[]{:S(2)}) collective-permute-start(bf16[1,16,32,512]{3,1,2,0:T(8,128)(2,1)} %get-tuple-element.31), channel_id=1, source_target_pairs={{0,2},{1,3},{2,0},{3,1},{4,6},{5,7},{6,4},{7,5},{8,10},{9,11},{10,... | collective-permute-start | bytes 1572872 | tf_op jit(solution)/shard_map/ppermute | solution.py:40
  126.6 21.7 %collective-permute-start.15 = (bf16[1,16,32,512]{3,1,2,0:T(8,128)(2,1)}, bf16[1,16,32,512]{3,1,2,0:T(8,128)(2,1)S(1)}, u32[]{:S(2)}, u32[]{:S(2)}) collective-permute-start(bf16[1,16,32,512]{3,1,2,0:T(8,128)(2,1)} %get-tuple-element.30), channel_id=1, source_target_pairs={{0,3},{1,0},{2,1},{3,2},{4,7},{5,4},{6,5},{7,6},{8,11},{9,8},{10,9... | collective-permute-start | bytes 1572872 | tf_op jit(solution)/shard_map/ppermute | solution.py:40
  149.4 69.5 %all-to-all-start.2 = ((bf16[1,16,128,512]{3,2,0,1:T(8,128)(2,1)}), bf16[1,16,128,512]{3,2,0,1:T(8,128)(2,1)}, u32[]{:S(2)}, u32[]{:S(2)}) async-start(bf16[1,16,128,512]{3,2,0,1:T(8,128)(2,1)} %copy_dynamic-update-slice_fusion.8), calls=%async_computation.2 | async-start | bytes 4194304 | tf_op jit(solution)/shard_map/all_to_all | solution.py:29
  218.8 52.3 %all-to-all-start.1 = ((bf16[1,2,1024,512]{3,1,0,2:T(2,128)(2,1)}), bf16[1,2,1024,512]{3,1,0,2:T(2,128)(2,1)S(1)}, u32[]{:S(2)}, u32[]{:S(2)}) async-start(bf16[1,2,1024,512]{3,1,0,2:T(2,128)(2,1)} %copy.95), calls=%async_computation.1 | async-start | bytes 4194304 | tf_op jit(solution)/shard_map/all_to_all | solution.py:29
  271.2 1.3 copy-start.3
  272.5 52.5 %all-to-all-start.3 = ((bf16[1,2,1024,512]{3,1,0,2:T(2,128)(2,1)}), bf16[1,2,1024,512]{3,1,0,2:T(2,128)(2,1)}, u32[]{:S(2)}, u32[]{:S(2)}) async-start(bf16[1,2,1024,512]{3,1,0,2:T(2,128)(2,1)} %copy.106), calls=%async_computation.3 | async-start | bytes 4194304 | tf_op jit(solution)/shard_map/all_to_all | solution.py:29
  278.9 19.0 %copy-start.7 = (f32[2,3,3,3]{3,0,2,1:T(2,128)S(1)}, f32[2,3,3,3]{3,0,2,1:T(2,128)}, u32[]{:S(2)}) copy-start(f32[2,3,3,3]{3,0,2,1:T(2,128)} %param.11) | copy-start | bytes 652
  279.0 16.1 %collective-permute-start.6 = (bf16[16,1,512]{2,1,0:T(2,128)(2,1)S(1)}, bf16[16,1,512]{2,1,0:T(2,128)(2,1)S(1)}, u32[]{:S(2)}, u32[]{:S(2)}) collective-permute-start(bf16[16,1,512]{2,1,0:T(2,128)(2,1)S(1)} %get-tuple-element.38), channel_id=1, source_target_pairs={{0,4},{4,8},{8,12},{12,16},{16,20},{20,24},{24,28},{1,5},{5,9},{9,... | collective-permute-start | bytes 49160 | tf_op jit(solution)/shard_map/ppermute | solution.py:20
  282.8 12.3 %collective-permute-start.7 = (bf16[16,1,512]{2,1,0:T(2,128)(2,1)S(1)}, bf16[16,1,512]{2,1,0:T(2,128)(2,1)S(1)}, u32[]{:S(2)}, u32[]{:S(2)}) collective-permute-start(bf16[16,1,512]{2,1,0:T(2,128)(2,1)S(1)} %get-tuple-element.39), channel_id=1, source_target_pairs={{4,0},{8,4},{12,8},{16,12},{20,16},{24,20},{28,24},{5,1},{9,5},{13... | collective-permute-start | bytes 49160 | tf_op jit(solution)/shard_map/ppermute | solution.py:21
  295.1 32.1 %collective-permute-start.8 = (bf16[1,130,512]{2,1,0:T(8,128)(2,1)S(1)}, bf16[1,130,512]{2,1,0:T(8,128)(2,1)S(1)}, u32[]{:S(2)}, u32[]{:S(2)}) collective-permute-start(bf16[1,130,512]{2,1,0:T(8,128)(2,1)S(1)} %get-tuple-element.14), channel_id=1, source_target_pairs={{0,1},{1,2},{2,3},{4,5},{5,6},{6,7},{8,9},{9,10},{10,11},{12,13},{... | collective-permute-start | bytes 399368 | tf_op jit(solution)/shard_map/ppermute | solution.py:20
  296.4 30.8 %collective-permute-start.9 = (bf16[1,130,512]{2,1,0:T(8,128)(2,1)S(1)}, bf16[1,130,512]{2,1,0:T(8,128)(2,1)S(1)}, u32[]{:S(2)}, u32[]{:S(2)}) collective-permute-start(bf16[1,130,512]{2,1,0:T(8,128)(2,1)S(1)} %get-tuple-element.15), channel_id=1, source_target_pairs={{1,0},{2,1},{3,2},{5,4},{6,5},{7,6},{9,8},{10,9},{11,10},{13,12},{... | collective-permute-start | bytes 399368 | tf_op jit(solution)/shard_map/ppermute | solution.py:21
  327.2 46.3 %copy-start.1 = (f32[1,2,8,128,512]{4,3,1,2,0:T(8,128)}, f32[1,2,8,128,512]{4,3,1,2,0:T(8,128)S(1)}, u32[]{:S(2)}) copy-start(f32[1,2,8,128,512]{4,3,1,2,0:T(8,128)S(1)} %copy.107) | copy-start | bytes 12582916
  373.4 1.6 collective-permute-start.22
  373.5 16.1 %copy-start.5 = (f32[2,128,512]{2,1,0:T(8,128)S(1)}, f32[2,128,512]{2,1,0:T(8,128)}, u32[]{:S(2)}) copy-start(f32[2,128,512]{2,1,0:T(8,128)} %param.7) | copy-start | bytes 1572868
  374.7 15.1 %copy-start.2 = (f32[1,2,8,128,512]{4,3,1,2,0:T(8,128)S(1)}, f32[1,2,8,128,512]{4,3,1,2,0:T(8,128)}, u32[]{:S(2)}) copy-start(f32[1,2,8,128,512]{4,3,1,2,0:T(8,128)} %copy-done.1) | copy-start | bytes 12582916
  375.1 2.0 collective-permute-start.16
  375.3 9.1 %collective-permute-start.23 = (f32[128,512]{1,0:T(8,128)S(1)}, f32[128,512]{1,0:T(8,128)S(1)}, u32[]{:S(2)}, u32[]{:S(2)}) collective-permute-start(f32[128,512]{1,0:T(8,128)S(1)} %get-tuple-element.50), channel_id=1, source_target_pairs={{0,2},{1,3},{2,0},{3,1},{4,6},{5,7},{6,4},{7,5},{8,10},{9,11},{10,... | collective-permute-start | bytes 786440 | tf_op jit(solution)/shard_map/ppermute | solution.py:54
  377.2 12.4 %collective-permute-start.17 = (f32[128,512]{1,0:T(8,128)S(1)}, f32[128,512]{1,0:T(8,128)S(1)}, u32[]{:S(2)}, u32[]{:S(2)}) collective-permute-start(f32[128,512]{1,0:T(8,128)S(1)} %add.106), channel_id=1, source_target_pairs={{0,2},{1,3},{2,0},{3,1},{4,6},{5,7},{6,4},{7,5},{8,10},{9,11},{10,... | collective-permute-start | bytes 786440 | tf_op jit(solution)/shard_map/ppermute | solution.py:54
  393.0 79.9 %all-to-all-start.6 = ((bf16[1,16,128,512]{3,2,0,1:T(8,128)(2,1)}), bf16[1,16,128,512]{3,2,0,1:T(8,128)(2,1)}, u32[]{:S(2)}, u32[]{:S(2)}) async-start(bf16[1,16,128,512]{3,2,0,1:T(8,128)(2,1)} %get-tuple-element.53), calls=%async_computation.6 | async-start | bytes 4194304 | tf_op jit(solution)/shard_map/all_to_all | solution.py:29
  404.3 18.0 %collective-permute-start.18 = (bf16[2,16,1,512]{3,2,1,0:T(2,128)(2,1)S(1)}, bf16[2,16,1,512]{3,2,1,0:T(2,128)(2,1)S(1)}, u32[]{:S(2)}, u32[]{:S(2)}) collective-permute-start(bf16[2,16,1,512]{3,2,1,0:T(2,128)(2,1)S(1)} %get-tuple-element.10), channel_id=1, source_target_pairs={{0,4},{4,8},{8,12},{12,16},{16,20},{20,24},{24,28},{1,5},{5,9},{9,... | collective-permute-start | bytes 98312 | tf_op jit(solution)/shard_map/ppermute | solution.py:20
  408.2 14.0 %collective-permute-start.19 = (bf16[2,16,1,512]{3,2,1,0:T(2,128)(2,1)S(1)}, bf16[2,16,1,512]{3,2,1,0:T(2,128)(2,1)S(1)}, u32[]{:S(2)}, u32[]{:S(2)}) collective-permute-start(bf16[2,16,1,512]{3,2,1,0:T(2,128)(2,1)S(1)} %get-tuple-element.11), channel_id=1, source_target_pairs={{4,0},{8,4},{12,8},{16,12},{20,16},{24,20},{28,24},{5,1},{9,5},{13... | collective-permute-start | bytes 98312 | tf_op jit(solution)/shard_map/ppermute | solution.py:21
  422.4 2.6 collective-permute-start.20
  423.7 4.3 collective-permute-start.21
  473.0 81.3 %all-to-all-start.4 = ((bf16[1,16,128,512]{3,2,0,1:T(8,128)(2,1)}), bf16[1,16,128,512]{3,2,0,1:T(8,128)(2,1)S(1)}, u32[]{:S(2)}, u32[]{:S(2)}) async-start(bf16[1,16,128,512]{3,2,0,1:T(8,128)(2,1)} %bitcast.48), calls=%async_computation.4 | async-start | bytes 4194304 | tf_op jit(solution)/shard_map/all_to_all | solution.py:29
  554.3 1.3 copy-start.4
  555.6 55.2 %all-to-all-start.7 = ((bf16[1,2,1024,512]{3,1,0,2:T(2,128)(2,1)}), bf16[1,2,1024,512]{3,1,0,2:T(2,128)(2,1)S(1)}, u32[]{:S(2)}, u32[]{:S(2)}) async-start(bf16[1,2,1024,512]{3,1,0,2:T(2,128)(2,1)} %copy.119), calls=%async_computation.7 | async-start | bytes 4194304 | tf_op jit(solution)/shard_map/all_to_all | solution.py:29
  610.8 52.6 %all-to-all-start.5 = ((bf16[1,2,1024,512]{3,1,0,2:T(2,128)(2,1)}), bf16[1,2,1024,512]{3,1,0,2:T(2,128)(2,1)}, u32[]{:S(2)}, u32[]{:S(2)}) async-start(bf16[1,2,1024,512]{3,1,0,2:T(2,128)(2,1)} %copy.110), calls=%async_computation.5 | async-start | bytes 4194304 | tf_op jit(solution)/shard_map/all_to_all | solution.py:29
  622.9 49.1 %collective-permute-start.30 = (bf16[1,16,32,512]{3,1,2,0:T(8,128)(2,1)}, bf16[1,16,32,512]{3,1,2,0:T(8,128)(2,1)}, u32[]{:S(2)}, u32[]{:S(2)}) collective-permute-start(bf16[1,16,32,512]{3,1,2,0:T(8,128)(2,1)} %get-tuple-element.29), channel_id=1, source_target_pairs={{0,1},{1,2},{2,3},{3,0},{4,5},{5,6},{6,7},{7,4},{8,9},{9,10},{10,1... | collective-permute-start | bytes 1572872 | tf_op jit(solution)/shard_map/ppermute | solution.py:40
  623.7 52.0 %collective-permute-start.31 = (bf16[1,16,32,512]{3,1,2,0:T(8,128)(2,1)}, bf16[1,16,32,512]{3,1,2,0:T(8,128)(2,1)}, u32[]{:S(2)}, u32[]{:S(2)}) collective-permute-start(bf16[1,16,32,512]{3,1,2,0:T(8,128)(2,1)} %get-tuple-element.28), channel_id=1, source_target_pairs={{0,2},{1,3},{2,0},{3,1},{4,6},{5,7},{6,4},{7,5},{8,10},{9,11},{10,... | collective-permute-start | bytes 1572872 | tf_op jit(solution)/shard_map/ppermute | solution.py:40
  623.7 53.8 %collective-permute-start.32 = (bf16[1,16,32,512]{3,1,2,0:T(8,128)(2,1)}, bf16[1,16,32,512]{3,1,2,0:T(8,128)(2,1)S(1)}, u32[]{:S(2)}, u32[]{:S(2)}) collective-permute-start(bf16[1,16,32,512]{3,1,2,0:T(8,128)(2,1)} %get-tuple-element.27), channel_id=1, source_target_pairs={{0,3},{1,0},{2,1},{3,2},{4,7},{5,4},{6,5},{7,6},{8,11},{9,8},{10,9... | collective-permute-start | bytes 1572872 | tf_op jit(solution)/shard_map/ppermute | solution.py:40
  671.6 13.3 %collective-permute-start.24 = (bf16[1,16,32,512]{3,1,2,0:T(8,128)(2,1)S(1)}, bf16[1,16,32,512]{3,1,2,0:T(8,128)(2,1)S(1)}, u32[]{:S(2)}, u32[]{:S(2)}) collective-permute-start(bf16[1,16,32,512]{3,1,2,0:T(8,128)(2,1)S(1)} %get-tuple-element.22), channel_id=1, source_target_pairs={{0,1},{1,2},{2,3},{3,0},{4,5},{5,6},{6,7},{7,4},{8,9},{9,10},{10,1... | collective-permute-start | bytes 1572872 | tf_op jit(solution)/shard_map/ppermute | solution.py:40
  671.9 14.8 %collective-permute-start.25 = (bf16[1,16,32,512]{3,1,2,0:T(8,128)(2,1)S(1)}, bf16[1,16,32,512]{3,1,2,0:T(8,128)(2,1)S(1)}, u32[]{:S(2)}, u32[]{:S(2)}) collective-permute-start(bf16[1,16,32,512]{3,1,2,0:T(8,128)(2,1)S(1)} %get-tuple-element.21), channel_id=1, source_target_pairs={{0,2},{1,3},{2,0},{3,1},{4,6},{5,7},{6,4},{7,5},{8,10},{9,11},{10,... | collective-permute-start | bytes 1572872 | tf_op jit(solution)/shard_map/ppermute | solution.py:40
  672.0 23.6 %collective-permute-start.26 = (bf16[1,16,32,512]{3,1,2,0:T(8,128)(2,1)S(1)}, bf16[1,16,32,512]{3,1,2,0:T(8,128)(2,1)S(1)}, u32[]{:S(2)}, u32[]{:S(2)}) collective-permute-start(bf16[1,16,32,512]{3,1,2,0:T(8,128)(2,1)S(1)} %get-tuple-element.20), channel_id=1, source_target_pairs={{0,3},{1,0},{2,1},{3,2},{4,7},{5,4},{6,5},{7,6},{8,11},{9,8},{10,9... | collective-permute-start | bytes 1572872 | tf_op jit(solution)/shard_map/ppermute | solution.py:40
  680.9 26.5 %collective-permute-start.33 = (bf16[1,16,32,512]{3,1,2,0:T(8,128)(2,1)S(1)}, bf16[1,16,32,512]{3,1,2,0:T(8,128)(2,1)S(1)}, u32[]{:S(2)}, u32[]{:S(2)}) collective-permute-start(bf16[1,16,32,512]{3,1,2,0:T(8,128)(2,1)S(1)} %get-tuple-element.25), channel_id=1, source_target_pairs={{0,1},{1,2},{2,3},{3,0},{4,5},{5,6},{6,7},{7,4},{8,9},{9,10},{10,1... | collective-permute-start | bytes 1572872 | tf_op jit(solution)/shard_map/ppermute | solution.py:40
  681.0 28.2 %collective-permute-start.34 = (bf16[1,16,32,512]{3,1,2,0:T(8,128)(2,1)S(1)}, bf16[1,16,32,512]{3,1,2,0:T(8,128)(2,1)S(1)}, u32[]{:S(2)}, u32[]{:S(2)}) collective-permute-start(bf16[1,16,32,512]{3,1,2,0:T(8,128)(2,1)S(1)} %get-tuple-element.24), channel_id=1, source_target_pairs={{0,2},{1,3},{2,0},{3,1},{4,6},{5,7},{6,4},{7,5},{8,10},{9,11},{10,... | collective-permute-start | bytes 1572872 | tf_op jit(solution)/shard_map/ppermute | solution.py:40
  684.9 33.2 %collective-permute-start.35 = (bf16[1,16,32,512]{3,1,2,0:T(8,128)(2,1)S(1)}, bf16[1,16,32,512]{3,1,2,0:T(8,128)(2,1)S(1)}, u32[]{:S(2)}, u32[]{:S(2)}) collective-permute-start(bf16[1,16,32,512]{3,1,2,0:T(8,128)(2,1)S(1)} %get-tuple-element.23), channel_id=1, source_target_pairs={{0,3},{1,0},{2,1},{3,2},{4,7},{5,4},{6,5},{7,6},{8,11},{9,8},{10,9... | collective-permute-start | bytes 1572872 | tf_op jit(solution)/shard_map/ppermute | solution.py:40
  695.6 22.8 %slice-start = ((s8[8388608]{0:T(1024)(128)(4,1)}), s8[4194304]{0:T(1024)(128)(4,1)S(1)}, s32[]{:S(2)}) async-start(s8[8388608]{0:T(1024)(128)(4,1)} %bitcast.241), calls=%async_computation.9 | async-start | bytes 8388608
  696.4 22.0 %slice-start.1 = ((s8[8388608]{0:T(1024)(128)(4,1)}), s8[4194304]{0:T(1024)(128)(4,1)S(1)}, s32[]{:S(2)}) async-start(s8[8388608]{0:T(1024)(128)(4,1)} %bitcast.241), calls=%async_computation.10 | async-start | bytes 8388608
  696.6 33.2 %collective-permute-start.27 = (bf16[1,16,32,512]{3,1,2,0:T(8,128)(2,1)S(1)}, bf16[1,16,32,512]{3,1,2,0:T(8,128)(2,1)S(1)}, u32[]{:S(2)}, u32[]{:S(2)}) collective-permute-start(bf16[1,16,32,512]{3,1,2,0:T(8,128)(2,1)S(1)} %get-tuple-element.18), channel_id=1, source_target_pairs={{0,1},{1,2},{2,3},{3,0},{4,5},{5,6},{6,7},{7,4},{8,9},{9,10},{10,1... | collective-permute-start | bytes 1572872 | tf_op jit(solution)/shard_map/ppermute | solution.py:40
  699.2 32.5 %collective-permute-start.28 = (bf16[1,16,32,512]{3,1,2,0:T(8,128)(2,1)S(1)}, bf16[1,16,32,512]{3,1,2,0:T(8,128)(2,1)S(1)}, u32[]{:S(2)}, u32[]{:S(2)}) collective-permute-start(bf16[1,16,32,512]{3,1,2,0:T(8,128)(2,1)S(1)} %get-tuple-element.17), channel_id=1, source_target_pairs={{0,2},{1,3},{2,0},{3,1},{4,6},{5,7},{6,4},{7,5},{8,10},{9,11},{10,... | collective-permute-start | bytes 1572872 | tf_op jit(solution)/shard_map/ppermute | solution.py:40
  707.4 30.7 %collective-permute-start.29 = (bf16[1,16,32,512]{3,1,2,0:T(8,128)(2,1)S(1)}, bf16[1,16,32,512]{3,1,2,0:T(8,128)(2,1)S(1)}, u32[]{:S(2)}, u32[]{:S(2)}) collective-permute-start(bf16[1,16,32,512]{3,1,2,0:T(8,128)(2,1)S(1)} %get-tuple-element.16), channel_id=1, source_target_pairs={{0,3},{1,0},{2,1},{3,2},{4,7},{5,4},{6,5},{7,6},{8,11},{9,8},{10,9... | collective-permute-start | bytes 1572872 | tf_op jit(solution)/shard_map/ppermute | solution.py:40
Sparse Core Ops, SparseCore 0:
  126.7 65.6 all-gather.1

commit v4 on v3

--- a/solution.py
+++ b/solution.py
@@ -42,6 +42,21 @@
     whole = jnp.zeros(shape, values.dtype)
     for owner, part in parts:
         whole = lax.dynamic_update_slice_in_dim(whole, part, owner * length, axis=concat)
+    return whole
+
+
+def gathered(values, axis):
+    peers, me = lax.axis_size(axis), lax.axis_index(axis)
+    if peers > 8:
+        return lax.all_gather(values, axis, axis=0, tiled=True)
+    rows = values.shape[0]
+    whole = jnp.zeros((rows * peers,) + values.shape[1:], values.dtype)
+    whole = lax.dynamic_update_slice_in_dim(whole, values, me * rows, axis=0)
+    for step in range(1, peers):
+        ring = [(i, (i + step) % peers) for i in range(peers)]
+        owner = lax.rem(me + peers - step, peers)
+        part = lax.ppermute(values, axis, ring)
+        whole = lax.dynamic_update_slice_in_dim(whole, part, owner * rows, axis=0)
     return whole
 
 
@@ -190,7 +205,7 @@
 
 def local(whitened, observed, lower_x, lower_y, lower_z, coupling_kernel):
     factor_x, factor_y = (
-        lax.all_gather(lower_x, "gx", axis=0, tiled=True),
+        gathered(lower_x, "gx"),
         lax.all_gather(lower_y, "gx", axis=0, tiled=True),
     )
 

time: 765 us -> 800 us (1.046)
  starting transfers between devices: 115 us -> 141 us
  waiting for transfers between devices: 325 us -> 341 us
  between operations: 15.1 us -> 1.77 us
    ppermute x0 -> x7, waiting for transfers between devices: none -> 59.5 us  [gathered(): part = lax.ppermute(values, axis, ring)]
    all_gather x1 -> x0, waiting for transfers between devices: 31.9 us -> none  [local(): lax.all_gather(lower_x, 'gx', axis=0, tiled=True)]
    all_to_all x8, waiting for transfers between devices: 160 us -> 146 us  [moved(): lax.all_to_all(values, axis, split_axis=split, concat_axis=concat, tiled=...]
    all_to_all x8, starting transfers between devices: 74.8 us -> 88.8 us  [moved(): lax.all_to_all(values, axis, split_axis=split, concat_axis=concat, tiled=...]
    ppermute x0 -> x7, starting transfers between devices: none -> 13 us  [gathered(): part = lax.ppermute(values, axis, ring)]
    dynamic_update_slice x0 -> x8, local copies, waits for them, and re-layouts: none -> 8.67 us  [the longest x7 7.97 us: gathered(): whole = lax.dynamic_update_slice_in_dim(whole, part, owner * rows, axis=0)]
  transfers between devices with their start and end apart: 45 -> 51, of which waited for: 31 -> 32; matrix products, arithmetic and copies ran while one was open for 19% -> 19% of each run, Pallas kernels for 6% -> 5%
where the time goes in v4:
time: 800 us; the launch traced here: 787 us
  waiting for transfers between devices  341 us (43%)
  starting transfers between devices  141 us (18%)
  local copies, waits for them, and re-layouts  129 us (16%)
  Pallas kernels  88.4 us (11%)
  matrix products  36.6 us (5%)
  blocking collectives  31.7 us (4%)
  other arithmetic  17.6 us (2%)
    all_to_all x8, waiting for transfers between devices, moved(): lax.all_to_all(values, axis, split_axis=split, concat_axis=concat, tiled=...  146 us
    ppermute x24, waiting for transfers between devices, moved(): sent = lax.ppermute(piece(lax.rem(me + step, peers)), axis, ring)  96.6 us
    all_to_all x8, starting transfers between devices, moved(): lax.all_to_all(values, axis, split_axis=split, concat_axis=concat, tiled=...  88.8 us
    ppermute x7, waiting for transfers between devices, gathered(): part = lax.ppermute(values, axis, ring)  59.5 us
    pallas_call x1, Pallas kernels, coupling_forward(): pl.pallas_call(forward_kernel, grid=(depth,), in_specs=[smem, smem, *plan...  45.2 us
    pallas_call x1, Pallas kernels, coupling_backward(): pl.pallas_call(backward_kernel, grid=(depth,), in_specs=[smem, smem, *pla...  43.2 us
    all_to_all x9, local copies, waits for them, and re-layouts, moved(): lax.all_to_all(values, axis, split_axis=split, concat_axis=concat, tiled=...  32 us
    all_gather x1, blocking collectives, local(): lax.all_gather(lower_y, 'gx', axis=0, tiled=True)  31.7 us
  transfers between devices with their start and end apart: 51, of which 32 were waited for; matrix products, arithmetic and copies ran while one was open for 19% of the time, Pallas kernels for 5%

profile of v4, /device:TPU:0, one launch (start us, length us, event | category | flops | bytes accessed | tf_op | source)
XLA Modules:
  0.0 786.5 jit_solution(12676525950115751898)
XLA Ops:
  0.7 4.0 convert_element_type.115
  12.4 31.7 %all_gather.3 = bf16[512,512]{1,0:T(8,128)(2,1)S(1)} all-gather(bf16[64,512]{1,0:T(8,128)(2,1)S(1)} %copy-done.7), channel_id=1, replica_groups=mesh['gx'=8,'gz'=4] {'gx'}, dimensions={0}, use_global_device_ids=true | all-gather | bytes 589824 | tf_op jit(solution)/shard_map/all_gather | solution.py:209
  47.2 3.1 fusion.46
  56.7 9.0 %collective-permute-done.3 = bf16[1,16,32,512]{3,1,2,0:T(8,128)(2,1)S(1)} collective-permute-done((bf16[1,16,32,512]{3,1,2,0:T(8,128)(2,1)S(1)}, bf16[1,16,32,512]{3,1,2,0:T(8,128)(2,1)S(1)}, u32[]{:S(2)}, u32[]{:S(2)}) %collective-permute-start.3) | collective-permute-done | bytes 524320 | tf_op jit(solution)/shard_map/ppermute | solution.py:40
  68.0 7.6 collective-permute-done.5
  76.7 5.5 all-to-all-start
  90.0 6.3 collective-permute-done.17
  97.4 3.3 collective-permute-done.18
  101.9 6.9 collective-permute-done.19
  109.9 4.8 fusion.49
  122.1 7.8 collective-permute-done.20
  133.5 6.9 collective-permute-done.22
  141.5 5.9 all-to-all-start.2
  159.4 33.5 %collective-permute-done.6 = bf16[128,1024]{1,0:T(8,128)(2,1)} collective-permute-done((bf16[128,1024]{1,0:T(8,128)(2,1)S(1)}, bf16[128,1024]{1,0:T(8,128)(2,1)}, u32[]{:S(2)}, u32[]{:S(2)}) %collective-permute-start.6) | collective-permute-done | bytes 262176 | tf_op jit(solution)/shard_map/ppermute | solution.py:58
  194.5 3.3 collective-permute-start.12
  199.6 26.0 %collective-permute-done.8 = bf16[128,1024]{1,0:T(8,128)(2,1)} collective-permute-done((bf16[128,1024]{1,0:T(8,128)(2,1)S(1)}, bf16[128,1024]{1,0:T(8,128)(2,1)}, u32[]{:S(2)}, u32[]{:S(2)}) %collective-permute-start.8) | collective-permute-done | bytes 262176 | tf_op jit(solution)/shard_map/ppermute | solution.py:58
  230.2 2.6 copy.94
  232.8 2.8 reshape.257
  235.6 5.3 convert_bitcast_fusion.3
  240.9 6.1 copy.95
  247.0 18.3 %all-to-all-start.1 = ((bf16[1,2,1024,512]{3,1,0,2:T(2,128)(2,1)}), bf16[1,2,1024,512]{3,1,0,2:T(2,128)(2,1)S(1)}, u32[]{:S(2)}, u32[]{:S(2)}) async-start(bf16[1,2,1024,512]{3,1,0,2:T(2,128)(2,1)} %copy.95), calls=%async_computation.1 | async-start | bytes 4194304 | tf_op jit(solution)/shard_map/all_to_all | solution.py:29
  265.3 4.3 copy.105
  269.7 4.2 reshape.266
  273.8 5.9 convert_bitcast_fusion.2
  279.7 6.1 copy.106
  285.9 28.0 %all-to-all-done.1 = bf16[1,2,1024,512]{3,1,0,2:T(2,128)(2,1)S(1)} async-done(((bf16[1,2,1024,512]{3,1,0,2:T(2,128)(2,1)}), bf16[1,2,1024,512]{3,1,0,2:T(2,128)(2,1)S(1)}, u32[]{:S(2)}, u32[]{:S(2)}) %all-to-all-start.1) | async-done | bytes 2097184 | tf_op jit(solution)/shard_map/all_to_all | solution.py:29
  315.2 4.3 all-to-all-start.3
  321.6 3.8 collective-permute-start.13
  326.7 10.8 %collective-permute-done.13 = bf16[16,1,512]{2,1,0:T(2,128)(2,1)S(1)} collective-permute-done((bf16[16,1,512]{2,1,0:T(2,128)(2,1)S(1)}, bf16[16,1,512]{2,1,0:T(2,128)(2,1)S(1)}, u32[]{:S(2)}, u32[]{:S(2)}) %collective-permute-start.13) | collective-permute-done | bytes 16416 | tf_op jit(solution)/shard_map/ppermute | solution.py:20
  340.6 27.1 %all-to-all-done.3 = bf16[1,2,1024,512]{3,1,0,2:T(2,128)(2,1)} async-done(((bf16[1,2,1024,512]{3,1,0,2:T(2,128)(2,1)}), bf16[1,2,1024,512]{3,1,0,2:T(2,128)(2,1)}, u32[]{:S(2)}, u32[]{:S(2)}) %all-to-all-start.3) | async-done | bytes 2097184 | tf_op jit(solution)/shard_map/all_to_all | solution.py:29
  370.9 45.2 %shard_map.77 = (f32[16,128,512]{2,1,0:T(8,128)S(1)}, f32[16,128,512]{2,1,0:T(8,128)S(1)}, f32[2,128,512]{2,1,0:T(8,128)S(1)}) custom-call(f32[54]{0:T(128)S(1)} %reshape.248.taps, f32[2,16]{1,0:T(2,128)S(1)} %pad_maximum_fusion.11.weights, f32[18,144,512]{2,1,0:T(8,128)S(1)} %fusion.15.p0.p1.p2, f32[18,144,512]{2,1,0:T(8,128)S(1)} %fusion.15.p0.p1.p2, ...), custom_call_target="tpu_custom_call" | custom-call | flops 1258291200 | bytes 25165824 | tf_op jit(solution)/shard_map/pallas_call | solution.py:168
  420.6 6.6 collective-permute-done.30
  427.2 5.0 collective-permute-done.24
  432.4 3.3 fusion.11
  435.7 9.9 %all-to-all-start.6 = ((bf16[1,16,128,512]{3,2,0,1:T(8,128)(2,1)}), bf16[1,16,128,512]{3,2,0,1:T(8,128)(2,1)}, u32[]{:S(2)}, u32[]{:S(2)}) async-start(bf16[1,16,128,512]{3,2,0,1:T(8,128)(2,1)} %get-tuple-element.53), calls=%async_computation.6 | async-start | bytes 4194304 | tf_op jit(solution)/shard_map/all_to_all | solution.py:29
  446.2 3.9 collective-permute-start.25
  451.4 12.7 %collective-permute-done.25 = bf16[2,16,1,512]{3,2,1,0:T(2,128)(2,1)S(1)} collective-permute-done((bf16[2,16,1,512]{3,2,1,0:T(2,128)(2,1)S(1)}, bf16[2,16,1,512]{3,2,1,0:T(2,128)(2,1)S(1)}, u32[]{:S(2)}, u32[]{:S(2)}) %collective-permute-start.25) | collective-permute-done | bytes 32800 | tf_op jit(solution)/shard_map/ppermute | solution.py:20
  466.9 3.0 collective-permute-done.28
  471.7 43.2 %shard_map.78 = bf16[16,128,512]{2,1,0:T(8,128)(2,1)} custom-call(f32[54]{0:T(128)S(1)} %reshape.248.taps, f32[2,16]{1,0:T(2,128)S(1)} %pad_maximum_fusion.11.weights, f32[2,18,144,512]{3,2,1,0:T(8,128)S(1)} %fusion.1.p0.p1.p2, f32[2,18,144,512]{3,2,1,0:T(8,128)S(1)} %fusion.1.p0.p1.p2, f32[2,18,144,512]{3,2,1,0:T(8,128)S(1)} %fusion.1.p0.p1.p2, ...), custom_call_target="tpu_custom_call" | custom-call | flops 1258291200 | bytes 33554432 | tf_op jit(solution)/shard_map/pallas_call | solution.py:184
  514.9 34.4 %all-to-all-start.4 = ((bf16[1,16,128,512]{3,2,0,1:T(8,128)(2,1)}), bf16[1,16,128,512]{3,2,0,1:T(8,128)(2,1)S(1)}, u32[]{:S(2)}, u32[]{:S(2)}) async-start(bf16[1,16,128,512]{3,2,0,1:T(8,128)(2,1)} %bitcast.48), calls=%async_computation.4 | async-start | bytes 4194304 | tf_op jit(solution)/shard_map/all_to_all | solution.py:29
  549.3 4.3 copy.118
  553.7 4.1 reshape.280
  557.8 5.9 convert_bitcast_fusion
  563.7 6.1 copy.119
  569.8 26.5 %all-to-all-done.4 = bf16[1,16,128,512]{3,2,0,1:T(8,128)(2,1)S(1)} async-done(((bf16[1,16,128,512]{3,2,0,1:T(8,128)(2,1)}), bf16[1,16,128,512]{3,2,0,1:T(8,128)(2,1)S(1)}, u32[]{:S(2)}, u32[]{:S(2)}) %all-to-all-start.4) | async-done | bytes 2097184 | tf_op jit(solution)/shard_map/all_to_all | solution.py:29
  597.6 6.2 all-to-all-start.7
  603.7 4.3 copy.109
  608.1 4.2 reshape.267
  612.2 5.9 convert_bitcast_fusion.1
  618.1 6.1 copy.110
  624.3 28.5 %all-to-all-done.7 = bf16[1,2,1024,512]{3,1,0,2:T(2,128)(2,1)S(1)} async-done(((bf16[1,2,1024,512]{3,1,0,2:T(2,128)(2,1)}), bf16[1,2,1024,512]{3,1,0,2:T(2,128)(2,1)S(1)}, u32[]{:S(2)}, u32[]{:S(2)}) %all-to-all-start.7) | async-done | bytes 2097184 | tf_op jit(solution)/shard_map/all_to_all | solution.py:29
  652.8 4.3 all-to-all-start.5
  657.1 3.7 copy.120
  660.8 2.7 all_to_all.111
  669.8 35.6 %all-to-all-done.5 = bf16[1,2,1024,512]{3,1,0,2:T(2,128)(2,1)} async-done(((bf16[1,2,1024,512]{3,1,0,2:T(2,128)(2,1)}), bf16[1,2,1024,512]{3,1,0,2:T(2,128)(2,1)}, u32[]{:S(2)}, u32[]{:S(2)}) %all-to-all-start.5) | async-done | bytes 2097184 | tf_op jit(solution)/shard_map/all_to_all | solution.py:29
  705.3 5.3 copy.111
  710.6 2.7 all_to_all.104
  728.8 8.8 %collective-permute-done.33 = bf16[1,16,32,512]{3,1,2,0:T(8,128)(2,1)S(1)} collective-permute-done((bf16[1,16,32,512]{3,1,2,0:T(8,128)(2,1)S(1)}, bf16[1,16,32,512]{3,1,2,0:T(8,128)(2,1)S(1)}, u32[]{:S(2)}, u32[]{:S(2)}) %collective-permute-start.33) | collective-permute-done | bytes 524320 | tf_op jit(solution)/shard_map/ppermute | solution.py:40
  738.6 2.6 collective-permute-start.34
  741.7 7.6 collective-permute-done.40
  751.5 8.5 %collective-permute-done.42 = bf16[1,16,32,512]{3,1,2,0:T(8,128)(2,1)S(1)} collective-permute-done((bf16[1,16,32,512]{3,1,2,0:T(8,128)(2,1)S(1)}, bf16[1,16,32,512]{3,1,2,0:T(8,128)(2,1)S(1)}, u32[]{:S(2)}, u32[]{:S(2)}) %collective-permute-start.42) | collective-permute-done | bytes 524320 | tf_op jit(solution)/shard_map/ppermute | solution.py:40
  761.7 10.1 %collective-permute-done.34 = bf16[1,16,32,512]{3,1,2,0:T(8,128)(2,1)S(1)} collective-permute-done((bf16[1,16,32,512]{3,1,2,0:T(8,128)(2,1)S(1)}, bf16[1,16,32,512]{3,1,2,0:T(8,128)(2,1)S(1)}, u32[]{:S(2)}, u32[]{:S(2)}) %collective-permute-start.34) | collective-permute-done | bytes 524320 | tf_op jit(solution)/shard_map/ppermute | solution.py:40
  774.0 6.1 collective-permute-done.36
  781.7 4.4 pad_maximum_fusion
  (171 shorter events, 117.7 us)
Async XLA Ops:
  0.6 46.5 %copy-start = (bf16[64,64]{1,0:T(8,128)(2,1)S(1)}, bf16[64,64]{1,0:T(8,128)(2,1)}, u32[]{:S(2)}) copy-start(bf16[64,64]{1,0:T(8,128)(2,1)} %param.10) | copy-start | bytes 24580
  7.4 5.0 copy-start.7
  7.4 36.6 %collective-permute-start = (bf16[1,16,32,512]{3,2,1,0:T(8,128)(2,1)}, bf16[1,16,32,512]{3,2,1,0:T(8,128)(2,1)}, u32[]{:S(2)}, u32[]{:S(2)}) collective-permute-start(bf16[1,16,32,512]{3,2,1,0:T(8,128)(2,1)} %get-tuple-element.46), channel_id=1, source_target_pairs={{0,1},{1,2},{2,3},{3,0},{4,5},{5,6},{6,7},{7,4},{8,9},{9,10},{10,1... | collective-permute-start | bytes 1572872 | tf_op jit(solution)/shard_map/ppermute | solution.py:40
  7.9 37.6 %collective-permute-start.1 = (bf16[1,16,32,512]{3,2,1,0:T(8,128)(2,1)}, bf16[1,16,32,512]{3,2,1,0:T(8,128)(2,1)}, u32[]{:S(2)}, u32[]{:S(2)}) collective-permute-start(bf16[1,16,32,512]{3,2,1,0:T(8,128)(2,1)} %get-tuple-element.45), channel_id=1, source_target_pairs={{0,2},{1,3},{2,0},{3,1},{4,6},{5,7},{6,4},{7,5},{8,10},{9,11},{10,... | collective-permute-start | bytes 1572872 | tf_op jit(solution)/shard_map/ppermute | solution.py:40
  10.4 36.4 %collective-permute-start.2 = (bf16[1,16,32,512]{3,2,1,0:T(8,128)(2,1)}, bf16[1,16,32,512]{3,2,1,0:T(8,128)(2,1)S(1)}, u32[]{:S(2)}, u32[]{:S(2)}) collective-permute-start(bf16[1,16,32,512]{3,2,1,0:T(8,128)(2,1)} %get-tuple-element.44), channel_id=1, source_target_pairs={{0,3},{1,0},{2,1},{3,2},{4,7},{5,4},{6,5},{7,6},{8,11},{9,8},{10,9... | collective-permute-start | bytes 1572872 | tf_op jit(solution)/shard_map/ppermute | solution.py:40
  52.0 13.7 %collective-permute-start.3 = (bf16[1,16,32,512]{3,1,2,0:T(8,128)(2,1)S(1)}, bf16[1,16,32,512]{3,1,2,0:T(8,128)(2,1)S(1)}, u32[]{:S(2)}, u32[]{:S(2)}) collective-permute-start(bf16[1,16,32,512]{3,1,2,0:T(8,128)(2,1)S(1)} %get-tuple-element.42), channel_id=1, source_target_pairs={{0,1},{1,2},{2,3},{3,0},{4,5},{5,6},{6,7},{7,4},{8,9},{9,10},{10,1... | collective-permute-start | bytes 1572872 | tf_op jit(solution)/shard_map/ppermute | solution.py:40
  52.1 14.8 %collective-permute-start.4 = (bf16[1,16,32,512]{3,1,2,0:T(8,128)(2,1)S(1)}, bf16[1,16,32,512]{3,1,2,0:T(8,128)(2,1)S(1)}, u32[]{:S(2)}, u32[]{:S(2)}) collective-permute-start(bf16[1,16,32,512]{3,1,2,0:T(8,128)(2,1)S(1)} %get-tuple-element.41), channel_id=1, source_target_pairs={{0,2},{1,3},{2,0},{3,1},{4,6},{5,7},{6,4},{7,5},{8,10},{9,11},{10,... | collective-permute-start | bytes 1572872 | tf_op jit(solution)/shard_map/ppermute | solution.py:40
  52.7 22.9 %collective-permute-start.5 = (bf16[1,16,32,512]{3,1,2,0:T(8,128)(2,1)S(1)}, bf16[1,16,32,512]{3,1,2,0:T(8,128)(2,1)S(1)}, u32[]{:S(2)}, u32[]{:S(2)}) collective-permute-start(bf16[1,16,32,512]{3,1,2,0:T(8,128)(2,1)S(1)} %get-tuple-element.40), channel_id=1, source_target_pairs={{0,3},{1,0},{2,1},{3,2},{4,7},{5,4},{6,5},{7,6},{8,11},{9,8},{10,9... | collective-permute-start | bytes 1572872 | tf_op jit(solution)/shard_map/ppermute | solution.py:40
  76.7 64.8 %all-to-all-start = ((bf16[1,16,128,512]{3,2,0,1:T(8,128)(2,1)}), bf16[1,16,128,512]{3,2,0,1:T(8,128)(2,1)S(1)}, u32[]{:S(2)}, u32[]{:S(2)}) async-start(bf16[1,16,128,512]{3,2,0,1:T(8,128)(2,1)} %copy_dynamic-update-slice_fusion.16), calls=%async_computation | async-start | bytes 4194304 | tf_op jit(solution)/shard_map/all_to_all | solution.py:29
  83.9 12.4 %collective-permute-start.17 = (bf16[1,16,32,512]{3,2,1,0:T(8,128)(2,1)S(1)}, bf16[1,16,32,512]{3,2,1,0:T(8,128)(2,1)S(1)}, u32[]{:S(2)}, u32[]{:S(2)}) collective-permute-start(bf16[1,16,32,512]{3,2,1,0:T(8,128)(2,1)S(1)} %get-tuple-element.36), channel_id=1, source_target_pairs={{0,1},{1,2},{2,3},{3,0},{4,5},{5,6},{6,7},{7,4},{8,9},{9,10},{10,1... | collective-permute-start | bytes 1572872 | tf_op jit(solution)/shard_map/ppermute | solution.py:40
  85.9 14.9 %collective-permute-start.18 = (bf16[1,16,32,512]{3,2,1,0:T(8,128)(2,1)S(1)}, bf16[1,16,32,512]{3,2,1,0:T(8,128)(2,1)S(1)}, u32[]{:S(2)}, u32[]{:S(2)}) collective-permute-start(bf16[1,16,32,512]{3,2,1,0:T(8,128)(2,1)S(1)} %get-tuple-element.35), channel_id=1, source_target_pairs={{0,2},{1,3},{2,0},{3,1},{4,6},{5,7},{6,4},{7,5},{8,10},{9,11},{10,... | collective-permute-start | bytes 1572872 | tf_op jit(solution)/shard_map/ppermute | solution.py:40
  86.4 22.3 %collective-permute-start.19 = (bf16[1,16,32,512]{3,2,1,0:T(8,128)(2,1)S(1)}, bf16[1,16,32,512]{3,2,1,0:T(8,128)(2,1)S(1)}, u32[]{:S(2)}, u32[]{:S(2)}) collective-permute-start(bf16[1,16,32,512]{3,2,1,0:T(8,128)(2,1)S(1)} %get-tuple-element.34), channel_id=1, source_target_pairs={{0,3},{1,0},{2,1},{3,2},{4,7},{5,4},{6,5},{7,6},{8,11},{9,8},{10,9... | collective-permute-start | bytes 1572872 | tf_op jit(solution)/shard_map/ppermute | solution.py:40
  116.4 13.5 %collective-permute-start.20 = (bf16[1,16,32,512]{3,1,2,0:T(8,128)(2,1)S(1)}, bf16[1,16,32,512]{3,1,2,0:T(8,128)(2,1)S(1)}, u32[]{:S(2)}, u32[]{:S(2)}) collective-permute-start(bf16[1,16,32,512]{3,1,2,0:T(8,128)(2,1)S(1)} %get-tuple-element.32), channel_id=1, source_target_pairs={{0,1},{1,2},{2,3},{3,0},{4,5},{5,6},{6,7},{7,4},{8,9},{9,10},{10,1... | collective-permute-start | bytes 1572872 | tf_op jit(solution)/shard_map/ppermute | solution.py:40
  117.5 14.8 %collective-permute-start.21 = (bf16[1,16,32,512]{3,1,2,0:T(8,128)(2,1)S(1)}, bf16[1,16,32,512]{3,1,2,0:T(8,128)(2,1)S(1)}, u32[]{:S(2)}, u32[]{:S(2)}) collective-permute-start(bf16[1,16,32,512]{3,1,2,0:T(8,128)(2,1)S(1)} %get-tuple-element.31), channel_id=1, source_target_pairs={{0,2},{1,3},{2,0},{3,1},{4,6},{5,7},{6,4},{7,5},{8,10},{9,11},{10,... | collective-permute-start | bytes 1572872 | tf_op jit(solution)/shard_map/ppermute | solution.py:40
  119.0 21.4 %collective-permute-start.22 = (bf16[1,16,32,512]{3,1,2,0:T(8,128)(2,1)S(1)}, bf16[1,16,32,512]{3,1,2,0:T(8,128)(2,1)S(1)}, u32[]{:S(2)}, u32[]{:S(2)}) collective-permute-start(bf16[1,16,32,512]{3,1,2,0:T(8,128)(2,1)S(1)} %get-tuple-element.30), channel_id=1, source_target_pairs={{0,3},{1,0},{2,1},{3,2},{4,7},{5,4},{6,5},{7,6},{8,11},{9,8},{10,9... | collective-permute-start | bytes 1572872 | tf_op jit(solution)/shard_map/ppermute | solution.py:40
  141.5 5.9 copy-start.6
  141.5 105.5 %all-to-all-start.2 = ((bf16[1,16,128,512]{3,2,0,1:T(8,128)(2,1)}), bf16[1,16,128,512]{3,2,0,1:T(8,128)(2,1)}, u32[]{:S(2)}, u32[]{:S(2)}) async-start(bf16[1,16,128,512]{3,2,0,1:T(8,128)(2,1)} %copy_dynamic-update-slice_fusion.8), calls=%async_computation.2 | async-start | bytes 4194304 | tf_op jit(solution)/shard_map/all_to_all | solution.py:29
  147.3 45.6 %collective-permute-start.6 = (bf16[128,1024]{1,0:T(8,128)(2,1)S(1)}, bf16[128,1024]{1,0:T(8,128)(2,1)}, u32[]{:S(2)}, u32[]{:S(2)}) collective-permute-start(bf16[128,1024]{1,0:T(8,128)(2,1)S(1)} %copy-done.6), channel_id=1, source_target_pairs={{0,4},{4,8},{8,12},{12,16},{16,20},{20,24},{24,28},{28,0},{1,5},{5... | collective-permute-start | bytes 786440 | tf_op jit(solution)/shard_map/ppermute | solution.py:58
  149.4 45.2 %collective-permute-start.7 = (bf16[128,1024]{1,0:T(8,128)(2,1)S(1)}, bf16[128,1024]{1,0:T(8,128)(2,1)}, u32[]{:S(2)}, u32[]{:S(2)}) collective-permute-start(bf16[128,1024]{1,0:T(8,128)(2,1)S(1)} %copy-done.6), channel_id=1, source_target_pairs={{0,8},{4,12},{8,16},{12,20},{16,24},{20,28},{24,0},{28,4},{1,9},{5... | collective-permute-start | bytes 786440 | tf_op jit(solution)/shard_map/ppermute | solution.py:58
  150.8 74.7 %collective-permute-start.8 = (bf16[128,1024]{1,0:T(8,128)(2,1)S(1)}, bf16[128,1024]{1,0:T(8,128)(2,1)}, u32[]{:S(2)}, u32[]{:S(2)}) collective-permute-start(bf16[128,1024]{1,0:T(8,128)(2,1)S(1)} %copy-done.6), channel_id=1, source_target_pairs={{0,12},{4,16},{8,20},{12,24},{16,28},{20,0},{24,4},{28,8},{1,13},{... | collective-permute-start | bytes 786440 | tf_op jit(solution)/shard_map/ppermute | solution.py:58
  153.2 74.1 %collective-permute-start.9 = (bf16[128,1024]{1,0:T(8,128)(2,1)S(1)}, bf16[128,1024]{1,0:T(8,128)(2,1)S(1)}, u32[]{:S(2)}, u32[]{:S(2)}) collective-permute-start(bf16[128,1024]{1,0:T(8,128)(2,1)S(1)} %copy-done.6), channel_id=1, source_target_pairs={{0,16},{4,20},{8,24},{12,28},{16,0},{20,4},{24,8},{28,12},{1,17},{... | collective-permute-start | bytes 786440 | tf_op jit(solution)/shard_map/ppermute | solution.py:58
  154.6 73.3 %collective-permute-start.10 = (bf16[128,1024]{1,0:T(8,128)(2,1)S(1)}, bf16[128,1024]{1,0:T(8,128)(2,1)S(1)}, u32[]{:S(2)}, u32[]{:S(2)}) collective-permute-start(bf16[128,1024]{1,0:T(8,128)(2,1)S(1)} %copy-done.6), channel_id=1, source_target_pairs={{0,20},{4,24},{8,28},{12,0},{16,4},{20,8},{24,12},{28,16},{1,21},{... | collective-permute-start | bytes 786440 | tf_op jit(solution)/shard_map/ppermute | solution.py:58
  192.9 35.8 %collective-permute-start.11 = (bf16[128,1024]{1,0:T(8,128)(2,1)S(1)}, bf16[128,1024]{1,0:T(8,128)(2,1)S(1)}, u32[]{:S(2)}, u32[]{:S(2)}) collective-permute-start(bf16[128,1024]{1,0:T(8,128)(2,1)S(1)} %copy-done.6), channel_id=1, source_target_pairs={{0,24},{4,28},{8,0},{12,4},{16,8},{20,12},{24,16},{28,20},{1,25},{... | collective-permute-start | bytes 786440 | tf_op jit(solution)/shard_map/ppermute | solution.py:58
  194.5 34.9 %collective-permute-start.12 = (bf16[128,1024]{1,0:T(8,128)(2,1)S(1)}, bf16[128,1024]{1,0:T(8,128)(2,1)S(1)}, u32[]{:S(2)}, u32[]{:S(2)}) collective-permute-start(bf16[128,1024]{1,0:T(8,128)(2,1)S(1)} %copy-done.6), channel_id=1, source_target_pairs={{0,28},{4,0},{8,4},{12,8},{16,12},{20,16},{24,20},{28,24},{1,29},{... | collective-permute-start | bytes 786440 | tf_op jit(solution)/shard_map/ppermute | solution.py:58
  247.0 66.8 %all-to-all-start.1 = ((bf16[1,2,1024,512]{3,1,0,2:T(2,128)(2,1)}), bf16[1,2,1024,512]{3,1,0,2:T(2,128)(2,1)S(1)}, u32[]{:S(2)}, u32[]{:S(2)}) async-start(bf16[1,2,1024,512]{3,1,0,2:T(2,128)(2,1)} %copy.95), calls=%async_computation.1 | async-start | bytes 4194304 | tf_op jit(solution)/shard_map/all_to_all | solution.py:29
  313.8 1.3 copy-start.3
  315.2 52.5 %all-to-all-start.3 = ((bf16[1,2,1024,512]{3,1,0,2:T(2,128)(2,1)}), bf16[1,2,1024,512]{3,1,0,2:T(2,128)(2,1)}, u32[]{:S(2)}, u32[]{:S(2)}) async-start(bf16[1,2,1024,512]{3,1,0,2:T(2,128)(2,1)} %copy.106), calls=%async_computation.3 | async-start | bytes 4194304 | tf_op jit(solution)/shard_map/all_to_all | solution.py:29
  321.5 18.9 %copy-start.8 = (f32[2,3,3,3]{3,0,2,1:T(2,128)S(1)}, f32[2,3,3,3]{3,0,2,1:T(2,128)}, u32[]{:S(2)}) copy-start(f32[2,3,3,3]{3,0,2,1:T(2,128)} %param.11) | copy-start | bytes 652
  321.6 16.0 %collective-permute-start.13 = (bf16[16,1,512]{2,1,0:T(2,128)(2,1)S(1)}, bf16[16,1,512]{2,1,0:T(2,128)(2,1)S(1)}, u32[]{:S(2)}, u32[]{:S(2)}) collective-permute-start(bf16[16,1,512]{2,1,0:T(2,128)(2,1)S(1)} %get-tuple-element.38), channel_id=1, source_target_pairs={{0,4},{4,8},{8,12},{12,16},{16,20},{20,24},{24,28},{1,5},{5,9},{9,... | collective-permute-start | bytes 49160 | tf_op jit(solution)/shard_map/ppermute | solution.py:20
  325.4 12.2 %collective-permute-start.14 = (bf16[16,1,512]{2,1,0:T(2,128)(2,1)S(1)}, bf16[16,1,512]{2,1,0:T(2,128)(2,1)S(1)}, u32[]{:S(2)}, u32[]{:S(2)}) collective-permute-start(bf16[16,1,512]{2,1,0:T(2,128)(2,1)S(1)} %get-tuple-element.39), channel_id=1, source_target_pairs={{4,0},{8,4},{12,8},{16,12},{20,16},{24,20},{28,24},{5,1},{9,5},{13... | collective-permute-start | bytes 49160 | tf_op jit(solution)/shard_map/ppermute | solution.py:21
  337.6 32.3 %collective-permute-start.15 = (bf16[1,130,512]{2,1,0:T(8,128)(2,1)S(1)}, bf16[1,130,512]{2,1,0:T(8,128)(2,1)S(1)}, u32[]{:S(2)}, u32[]{:S(2)}) collective-permute-start(bf16[1,130,512]{2,1,0:T(8,128)(2,1)S(1)} %get-tuple-element.14), channel_id=1, source_target_pairs={{0,1},{1,2},{2,3},{4,5},{5,6},{6,7},{8,9},{9,10},{10,11},{12,13},{... | collective-permute-start | bytes 399368 | tf_op jit(solution)/shard_map/ppermute | solution.py:20
  339.0 31.0 %collective-permute-start.16 = (bf16[1,130,512]{2,1,0:T(8,128)(2,1)S(1)}, bf16[1,130,512]{2,1,0:T(8,128)(2,1)S(1)}, u32[]{:S(2)}, u32[]{:S(2)}) collective-permute-start(bf16[1,130,512]{2,1,0:T(8,128)(2,1)S(1)} %get-tuple-element.15), channel_id=1, source_target_pairs={{1,0},{2,1},{3,2},{5,4},{6,5},{7,6},{9,8},{10,9},{11,10},{13,12},{... | collective-permute-start | bytes 399368 | tf_op jit(solution)/shard_map/ppermute | solution.py:21
  369.9 46.3 %copy-start.1 = (f32[1,2,8,128,512]{4,3,1,2,0:T(8,128)}, f32[1,2,8,128,512]{4,3,1,2,0:T(8,128)S(1)}, u32[]{:S(2)}) copy-start(f32[1,2,8,128,512]{4,3,1,2,0:T(8,128)S(1)} %copy.107) | copy-start | bytes 12582916
  416.1 1.6 collective-permute-start.29
  416.2 16.0 %copy-start.5 = (f32[2,128,512]{2,1,0:T(8,128)S(1)}, f32[2,128,512]{2,1,0:T(8,128)}, u32[]{:S(2)}) copy-start(f32[2,128,512]{2,1,0:T(8,128)} %param.7) | copy-start | bytes 1572868
  417.4 15.0 %copy-start.2 = (f32[1,2,8,128,512]{4,3,1,2,0:T(8,128)S(1)}, f32[1,2,8,128,512]{4,3,1,2,0:T(8,128)}, u32[]{:S(2)}) copy-start(f32[1,2,8,128,512]{4,3,1,2,0:T(8,128)} %copy-done.1) | copy-start | bytes 12582916
  417.8 1.6 collective-permute-start.23
  418.0 9.1 %collective-permute-start.30 = (f32[128,512]{1,0:T(8,128)S(1)}, f32[128,512]{1,0:T(8,128)S(1)}, u32[]{:S(2)}, u32[]{:S(2)}) collective-permute-start(f32[128,512]{1,0:T(8,128)S(1)} %get-tuple-element.50), channel_id=1, source_target_pairs={{0,2},{1,3},{2,0},{3,1},{4,6},{5,7},{6,4},{7,5},{8,10},{9,11},{10,... | collective-permute-start | bytes 786440 | tf_op jit(solution)/shard_map/ppermute | solution.py:69
  419.5 12.8 %collective-permute-start.24 = (f32[128,512]{1,0:T(8,128)S(1)}, f32[128,512]{1,0:T(8,128)S(1)}, u32[]{:S(2)}, u32[]{:S(2)}) collective-permute-start(f32[128,512]{1,0:T(8,128)S(1)} %add.289), channel_id=1, source_target_pairs={{0,2},{1,3},{2,0},{3,1},{4,6},{5,7},{6,4},{7,5},{8,10},{9,11},{10,... | collective-permute-start | bytes 786440 | tf_op jit(solution)/shard_map/ppermute | solution.py:69
  435.7 79.2 %all-to-all-start.6 = ((bf16[1,16,128,512]{3,2,0,1:T(8,128)(2,1)}), bf16[1,16,128,512]{3,2,0,1:T(8,128)(2,1)}, u32[]{:S(2)}, u32[]{:S(2)}) async-start(bf16[1,16,128,512]{3,2,0,1:T(8,128)(2,1)} %get-tuple-element.53), calls=%async_computation.6 | async-start | bytes 4194304 | tf_op jit(solution)/shard_map/all_to_all | solution.py:29
  446.2 18.0 %collective-permute-start.25 = (bf16[2,16,1,512]{3,2,1,0:T(2,128)(2,1)S(1)}, bf16[2,16,1,512]{3,2,1,0:T(2,128)(2,1)S(1)}, u32[]{:S(2)}, u32[]{:S(2)}) collective-permute-start(bf16[2,16,1,512]{3,2,1,0:T(2,128)(2,1)S(1)} %get-tuple-element.10), channel_id=1, source_target_pairs={{0,4},{4,8},{8,12},{12,16},{16,20},{20,24},{24,28},{1,5},{5,9},{9,... | collective-permute-start | bytes 98312 | tf_op jit(solution)/shard_map/ppermute | solution.py:20
  450.1 14.0 %collective-permute-start.26 = (bf16[2,16,1,512]{3,2,1,0:T(2,128)(2,1)S(1)}, bf16[2,16,1,512]{3,2,1,0:T(2,128)(2,1)S(1)}, u32[]{:S(2)}, u32[]{:S(2)}) collective-permute-start(bf16[2,16,1,512]{3,2,1,0:T(2,128)(2,1)S(1)} %get-tuple-element.11), channel_id=1, source_target_pairs={{4,0},{8,4},{12,8},{16,12},{20,16},{24,20},{28,24},{5,1},{9,5},{13... | collective-permute-start | bytes 98312 | tf_op jit(solution)/shard_map/ppermute | solution.py:21
  464.3 2.6 collective-permute-start.27
  465.6 4.3 collective-permute-start.28
  514.9 81.3 %all-to-all-start.4 = ((bf16[1,16,128,512]{3,2,0,1:T(8,128)(2,1)}), bf16[1,16,128,512]{3,2,0,1:T(8,128)(2,1)S(1)}, u32[]{:S(2)}, u32[]{:S(2)}) async-start(bf16[1,16,128,512]{3,2,0,1:T(8,128)(2,1)} %bitcast.48), calls=%async_computation.4 | async-start | bytes 4194304 | tf_op jit(solution)/shard_map/all_to_all | solution.py:29
  596.2 1.3 copy-start.4
  597.6 55.2 %all-to-all-start.7 = ((bf16[1,2,1024,512]{3,1,0,2:T(2,128)(2,1)}), bf16[1,2,1024,512]{3,1,0,2:T(2,128)(2,1)S(1)}, u32[]{:S(2)}, u32[]{:S(2)}) async-start(bf16[1,2,1024,512]{3,1,0,2:T(2,128)(2,1)} %copy.119), calls=%async_computation.7 | async-start | bytes 4194304 | tf_op jit(solution)/shard_map/all_to_all | solution.py:29
  652.8 52.6 %all-to-all-start.5 = ((bf16[1,2,1024,512]{3,1,0,2:T(2,128)(2,1)}), bf16[1,2,1024,512]{3,1,0,2:T(2,128)(2,1)}, u32[]{:S(2)}, u32[]{:S(2)}) async-start(bf16[1,2,1024,512]{3,1,0,2:T(2,128)(2,1)} %copy.110), calls=%async_computation.5 | async-start | bytes 4194304 | tf_op jit(solution)/shard_map/all_to_all | solution.py:29
  664.8 49.2 %collective-permute-start.37 = (bf16[1,16,32,512]{3,1,2,0:T(8,128)(2,1)}, bf16[1,16,32,512]{3,1,2,0:T(8,128)(2,1)}, u32[]{:S(2)}, u32[]{:S(2)}) collective-permute-start(bf16[1,16,32,512]{3,1,2,0:T(8,128)(2,1)} %get-tuple-element.29), channel_id=1, source_target_pairs={{0,1},{1,2},{2,3},{3,0},{4,5},{5,6},{6,7},{7,4},{8,9},{9,10},{10,1... | collective-permute-start | bytes 1572872 | tf_op jit(solution)/shard_map/ppermute | solution.py:40
  665.6 52.0 %collective-permute-start.38 = (bf16[1,16,32,512]{3,1,2,0:T(8,128)(2,1)}, bf16[1,16,32,512]{3,1,2,0:T(8,128)(2,1)}, u32[]{:S(2)}, u32[]{:S(2)}) collective-permute-start(bf16[1,16,32,512]{3,1,2,0:T(8,128)(2,1)} %get-tuple-element.28), channel_id=1, source_target_pairs={{0,2},{1,3},{2,0},{3,1},{4,6},{5,7},{6,4},{7,5},{8,10},{9,11},{10,... | collective-permute-start | bytes 1572872 | tf_op jit(solution)/shard_map/ppermute | solution.py:40
  665.6 53.9 %collective-permute-start.39 = (bf16[1,16,32,512]{3,1,2,0:T(8,128)(2,1)}, bf16[1,16,32,512]{3,1,2,0:T(8,128)(2,1)S(1)}, u32[]{:S(2)}, u32[]{:S(2)}) collective-permute-start(bf16[1,16,32,512]{3,1,2,0:T(8,128)(2,1)} %get-tuple-element.27), channel_id=1, source_target_pairs={{0,3},{1,0},{2,1},{3,2},{4,7},{5,4},{6,5},{7,6},{8,11},{9,8},{10,9... | collective-permute-start | bytes 1572872 | tf_op jit(solution)/shard_map/ppermute | solution.py:40
  713.5 13.3 %collective-permute-start.31 = (bf16[1,16,32,512]{3,1,2,0:T(8,128)(2,1)S(1)}, bf16[1,16,32,512]{3,1,2,0:T(8,128)(2,1)S(1)}, u32[]{:S(2)}, u32[]{:S(2)}) collective-permute-start(bf16[1,16,32,512]{3,1,2,0:T(8,128)(2,1)S(1)} %get-tuple-element.22), channel_id=1, source_target_pairs={{0,1},{1,2},{2,3},{3,0},{4,5},{5,6},{6,7},{7,4},{8,9},{9,10},{10,1... | collective-permute-start | bytes 1572872 | tf_op jit(solution)/shard_map/ppermute | solution.py:40
  713.8 14.8 %collective-permute-start.32 = (bf16[1,16,32,512]{3,1,2,0:T(8,128)(2,1)S(1)}, bf16[1,16,32,512]{3,1,2,0:T(8,128)(2,1)S(1)}, u32[]{:S(2)}, u32[]{:S(2)}) collective-permute-start(bf16[1,16,32,512]{3,1,2,0:T(8,128)(2,1)S(1)} %get-tuple-element.21), channel_id=1, source_target_pairs={{0,2},{1,3},{2,0},{3,1},{4,6},{5,7},{6,4},{7,5},{8,10},{9,11},{10,... | collective-permute-start | bytes 1572872 | tf_op jit(solution)/shard_map/ppermute | solution.py:40
  713.9 23.6 %collective-permute-start.33 = (bf16[1,16,32,512]{3,1,2,0:T(8,128)(2,1)S(1)}, bf16[1,16,32,512]{3,1,2,0:T(8,128)(2,1)S(1)}, u32[]{:S(2)}, u32[]{:S(2)}) collective-permute-start(bf16[1,16,32,512]{3,1,2,0:T(8,128)(2,1)S(1)} %get-tuple-element.20), channel_id=1, source_target_pairs={{0,3},{1,0},{2,1},{3,2},{4,7},{5,4},{6,5},{7,6},{8,11},{9,8},{10,9... | collective-permute-start | bytes 1572872 | tf_op jit(solution)/shard_map/ppermute | solution.py:40
  722.8 26.5 %collective-permute-start.40 = (bf16[1,16,32,512]{3,1,2,0:T(8,128)(2,1)S(1)}, bf16[1,16,32,512]{3,1,2,0:T(8,128)(2,1)S(1)}, u32[]{:S(2)}, u32[]{:S(2)}) collective-permute-start(bf16[1,16,32,512]{3,1,2,0:T(8,128)(2,1)S(1)} %get-tuple-element.25), channel_id=1, source_target_pairs={{0,1},{1,2},{2,3},{3,0},{4,5},{5,6},{6,7},{7,4},{8,9},{9,10},{10,1... | collective-permute-start | bytes 1572872 | tf_op jit(solution)/shard_map/ppermute | solution.py:40
  722.9 28.2 %collective-permute-start.41 = (bf16[1,16,32,512]{3,1,2,0:T(8,128)(2,1)S(1)}, bf16[1,16,32,512]{3,1,2,0:T(8,128)(2,1)S(1)}, u32[]{:S(2)}, u32[]{:S(2)}) collective-permute-start(bf16[1,16,32,512]{3,1,2,0:T(8,128)(2,1)S(1)} %get-tuple-element.24), channel_id=1, source_target_pairs={{0,2},{1,3},{2,0},{3,1},{4,6},{5,7},{6,4},{7,5},{8,10},{9,11},{10,... | collective-permute-start | bytes 1572872 | tf_op jit(solution)/shard_map/ppermute | solution.py:40
  726.8 33.2 %collective-permute-start.42 = (bf16[1,16,32,512]{3,1,2,0:T(8,128)(2,1)S(1)}, bf16[1,16,32,512]{3,1,2,0:T(8,128)(2,1)S(1)}, u32[]{:S(2)}, u32[]{:S(2)}) collective-permute-start(bf16[1,16,32,512]{3,1,2,0:T(8,128)(2,1)S(1)} %get-tuple-element.23), channel_id=1, source_target_pairs={{0,3},{1,0},{2,1},{3,2},{4,7},{5,4},{6,5},{7,6},{8,11},{9,8},{10,9... | collective-permute-start | bytes 1572872 | tf_op jit(solution)/shard_map/ppermute | solution.py:40
  737.5 22.8 %slice-start = ((s8[8388608]{0:T(1024)(128)(4,1)}), s8[4194304]{0:T(1024)(128)(4,1)S(1)}, s32[]{:S(2)}) async-start(s8[8388608]{0:T(1024)(128)(4,1)} %bitcast.241), calls=%async_computation.8 | async-start | bytes 8388608
  738.3 22.0 %slice-start.1 = ((s8[8388608]{0:T(1024)(128)(4,1)}), s8[4194304]{0:T(1024)(128)(4,1)S(1)}, s32[]{:S(2)}) async-start(s8[8388608]{0:T(1024)(128)(4,1)} %bitcast.241), calls=%async_computation.9 | async-start | bytes 8388608
  738.6 33.2 %collective-permute-start.34 = (bf16[1,16,32,512]{3,1,2,0:T(8,128)(2,1)S(1)}, bf16[1,16,32,512]{3,1,2,0:T(8,128)(2,1)S(1)}, u32[]{:S(2)}, u32[]{:S(2)}) collective-permute-start(bf16[1,16,32,512]{3,1,2,0:T(8,128)(2,1)S(1)} %get-tuple-element.18), channel_id=1, source_target_pairs={{0,1},{1,2},{2,3},{3,0},{4,5},{5,6},{6,7},{7,4},{8,9},{9,10},{10,1... | collective-permute-start | bytes 1572872 | tf_op jit(solution)/shard_map/ppermute | solution.py:40
  741.1 32.5 %collective-permute-start.35 = (bf16[1,16,32,512]{3,1,2,0:T(8,128)(2,1)S(1)}, bf16[1,16,32,512]{3,1,2,0:T(8,128)(2,1)S(1)}, u32[]{:S(2)}, u32[]{:S(2)}) collective-permute-start(bf16[1,16,32,512]{3,1,2,0:T(8,128)(2,1)S(1)} %get-tuple-element.17), channel_id=1, source_target_pairs={{0,2},{1,3},{2,0},{3,1},{4,6},{5,7},{6,4},{7,5},{8,10},{9,11},{10,... | collective-permute-start | bytes 1572872 | tf_op jit(solution)/shard_map/ppermute | solution.py:40
  749.3 30.7 %collective-permute-start.36 = (bf16[1,16,32,512]{3,1,2,0:T(8,128)(2,1)S(1)}, bf16[1,16,32,512]{3,1,2,0:T(8,128)(2,1)S(1)}, u32[]{:S(2)}, u32[]{:S(2)}) collective-permute-start(bf16[1,16,32,512]{3,1,2,0:T(8,128)(2,1)S(1)} %get-tuple-element.16), channel_id=1, source_target_pairs={{0,3},{1,0},{2,1},{3,2},{4,7},{5,4},{6,5},{7,6},{8,11},{9,8},{10,9... | collective-permute-start | bytes 1572872 | tf_op jit(solution)/shard_map/ppermute | solution.py:40
